TPU v7x, 128 devices: a whole 4x4x4 slice. The times are simulated.
128 devices in a mesh: fsdp: 16 (over z_hi, y, core), ctx: 2 (over z_lo), tp: 4 (over x).
Axes of the slice: x: 4, y: 4, z: 4 (z_hi: 2, z_lo: 2; z = z_hi * 2 + z_lo), core: 2. Of those that a mesh axis runs over, the one named last changes fastest.
Arguments:
- tokens: bfloat16 [16, 1536, 1024], P('fsdp', 'ctx'), may hold values from -6 to 6
- norm_gain: bfloat16 [1024], replicated, may hold values from 0.5 to 1.5
- in_weight: bfloat16 [1024, 3, 1024], P('fsdp', None, 'tp'), may hold values from -0.1875 to 0.1875
- conv_weight: bfloat16 [3, 1024], P(None, 'tp'), may hold values from -3 to 3
- out_weight: bfloat16 [1024, 1024], P('tp', 'fsdp'), may hold values from -0.1875 to 0.1875
- ffn_gain: bfloat16 [1024], replicated, may hold values from 0.5 to 1.5
- gate_up_weight: bfloat16 [2, 1024, 4608], P(None, 'fsdp', 'tp'), may hold values from -0.1875 to 0.1875
- down_weight: bfloat16 [4608, 1024], P('tp', 'fsdp'), may hold values from -0.125 to 0.125
- cotangent: bfloat16 [16, 1536, 1024], P('fsdp', 'ctx'), may hold values from -6 to 6
Outputs:
- output: bfloat16 [16, 1536, 1024], P('fsdp', 'ctx')
- input_grad: bfloat16 [16, 1536, 1024], P('fsdp', 'ctx')
- norm_gain_grad: float32 [1024], replicated
- in_weight_grad: float32 [1024, 3, 1024], P('fsdp', None, 'tp')
- conv_weight_grad: float32 [3, 1024], P(None, 'tp')
- out_weight_grad: float32 [1024, 1024], P('tp', 'fsdp')
- ffn_gain_grad: float32 [1024], replicated
- gate_up_grad: float32 [2, 1024, 4608], P(None, 'fsdp', 'tp')
- down_weight_grad: float32 [4608, 1024], P('tp', 'fsdp')
All inputs are finite; a program needn't handle non-finite values.
Results may differ from a plain program's by a relative error of at most 0.018.
Values may be sent and summed in bfloat16 or wider, within the bound.
No kernel may reach another device: no remote copies, remote signals or barrier semaphores. Data moves between devices by JAX's collectives and lax.ppermute only.
A program may use at most 128 MiB of HBM per device.

v0:
```python
import jax
import jax.numpy as jnp
from jax import lax
from jax.sharding import PartitionSpec as P

EPSILON = 1e-05


def passed_along(block, axis, distance):
    devices = range(lax.axis_size(axis))
    route = [(i - distance, i) for i in devices if i - distance in devices]
    return lax.ppermute(block, axis, route)


def rms_forward(inputs, gain_vec):
    inv_rms = lax.rsqrt(jnp.mean(inputs * inputs, axis=-1, keepdims=True) + EPSILON)
    normed = inputs * inv_rms
    return (normed, inv_rms, normed * gain_vec)


def rms_backward(incoming, normed, inv_rms, gain_vec):
    scaled = incoming * gain_vec
    inner = jnp.mean(scaled * normed, axis=-1, keepdims=True)
    return (inv_rms * (scaled - normed * inner), jnp.sum(incoming * normed, axis=0))


def body(
    tokens,
    norm_gain,
    in_weight,
    conv_weight,
    out_weight,
    ffn_gain,
    gate_up_weight,
    down_weight,
    cotangent,
):
    in_shape = tokens.shape
    model_width = in_shape[-1]
    token_rows = tokens.reshape(-1, model_width).astype(jnp.float32)
    row_count = token_rows.shape[0]
    first_gain = norm_gain.astype(jnp.float32)
    second_gain = ffn_gain.astype(jnp.float32)
    conv_taps = conv_weight.astype(jnp.float32)
    contract_rows = (((0,), (0,)), ((), ()))
    contract_cols = (((1,), (1,)), ((), ()))
    w_in, w_gu, w_out, w_down = (
        lax.all_gather(in_weight, "fsdp", axis=0, tiled=True),
        lax.all_gather(gate_up_weight, "fsdp", axis=1, tiled=True),
        lax.all_gather(out_weight, "fsdp", axis=1, tiled=True),
        lax.all_gather(down_weight, "fsdp", axis=1, tiled=True),
    )
    channels = w_in.shape[2]
    normed_one, inv_one, scaled_one = rms_forward(token_rows, first_gain)
    normed_in = scaled_one.astype(jnp.bfloat16)
    projected = jnp.dot(
        normed_in, w_in.reshape(model_width, 3 * channels), preferred_element_type=jnp.float32
    ).reshape(row_count, 3, channels)
    gate_b = projected[:, 0]
    gate_c = projected[:, 1]
    values_v = projected[:, 2]
    mixed_in = (gate_b * values_v).astype(jnp.bfloat16)
    arrived = passed_along(mixed_in[row_count - 2 :], "ctx", 1)
    extended = jnp.concatenate([arrived, mixed_in], 0).astype(jnp.float32)
    conv_out = (
        conv_taps[0] * extended[:row_count]
        + conv_taps[1] * extended[1 : row_count + 1]
        + conv_taps[2] * extended[2:]
    )
    gated = (gate_c * conv_out).astype(jnp.bfloat16)
    mixer_part = jnp.dot(gated, w_out, preferred_element_type=jnp.float32)
    middle = token_rows + lax.psum(mixer_part, "tp")
    normed_two, inv_two, scaled_two = rms_forward(middle, second_gain)
    normed_mid = scaled_two.astype(jnp.bfloat16)
    gate_up = jnp.einsum("rd,kdf->rkf", normed_mid, w_gu, preferred_element_type=jnp.float32)
    gate_g = gate_up[:, 0]
    up_u = gate_up[:, 1]
    sigmoid_g = jax.nn.sigmoid(gate_g)
    silu_g = gate_g * sigmoid_g
    activated = (silu_g * up_u).astype(jnp.bfloat16)
    ffn_part = jnp.dot(activated, w_down, preferred_element_type=jnp.float32)
    result = (
        (middle + lax.psum(ffn_part.astype(jnp.bfloat16), "tp").astype(jnp.float32))
        .astype(jnp.bfloat16)
        .reshape(in_shape)
    )
    w_in, w_gu, w_out, w_down = (
        lax.all_gather(in_weight, "fsdp", axis=0, tiled=True),
        lax.all_gather(gate_up_weight, "fsdp", axis=1, tiled=True),
        lax.all_gather(out_weight, "fsdp", axis=1, tiled=True),
        lax.all_gather(down_weight, "fsdp", axis=1, tiled=True),
    )
    grad_out = cotangent.reshape(-1, model_width)
    grad_down = lax.dot_general(
        activated, grad_out, contract_rows, preferred_element_type=jnp.float32
    )
    grad_act = lax.dot_general(grad_out, w_down, contract_cols, preferred_element_type=jnp.float32)
    grad_gate = (grad_act * up_u * sigmoid_g * (1.0 + gate_g * (1.0 - sigmoid_g))).astype(
        jnp.bfloat16
    )
    grad_up = (grad_act * silu_g).astype(jnp.bfloat16)
    grad_both = jnp.stack([grad_gate, grad_up], 1)
    grad_gu = jnp.einsum("rd,rkf->kdf", normed_mid, grad_both, preferred_element_type=jnp.float32)
    mid_part = jnp.einsum("rkf,kdf->rd", grad_both, w_gu, preferred_element_type=jnp.float32)
    grad_mid_in = lax.psum(mid_part, "tp")
    back_two, grad_gain_two = rms_backward(grad_mid_in, normed_two, inv_two, second_gain)
    grad_middle = grad_out.astype(jnp.float32) + back_two
    grad_branch = grad_middle.astype(jnp.bfloat16)
    grad_wout = lax.dot_general(
        gated, grad_branch, contract_rows, preferred_element_type=jnp.float32
    )
    grad_gated = lax.dot_general(
        grad_branch, w_out, contract_cols, preferred_element_type=jnp.float32
    )
    grad_cpart = grad_gated * conv_out
    grad_conv = grad_gated * gate_c
    grad_taps = jnp.stack(
        [
            jnp.sum(extended[:row_count] * grad_conv, 0),
            jnp.sum(extended[1 : row_count + 1] * grad_conv, 0),
            jnp.sum(extended[2:] * grad_conv, 0),
        ],
        0,
    )
    edge_zeros = jnp.zeros((2, channels), jnp.float32)
    padded = jnp.concatenate([edge_zeros, grad_conv, edge_zeros], 0)
    grad_ext = conv_taps[0] * padded[2:] + conv_taps[1] * padded[1:-1] + conv_taps[2] * padded[:-2]
    returned = passed_along(grad_ext[:2], "ctx", -1)
    grad_mixed = grad_ext[2:] + jnp.concatenate(
        [jnp.zeros((row_count - 2, channels), jnp.float32), returned], 0
    )
    rounded = grad_mixed.astype(jnp.bfloat16).astype(jnp.float32)
    grad_proj = jnp.stack([rounded * values_v, grad_cpart, rounded * gate_b], 1).astype(
        jnp.bfloat16
    )
    grad_win = jnp.einsum("rd,rkc->dkc", normed_in, grad_proj, preferred_element_type=jnp.float32)
    norm_part = jnp.einsum("rkc,dkc->rd", grad_proj, w_in, preferred_element_type=jnp.float32)
    grad_norm_in = lax.psum(norm_part.astype(jnp.bfloat16), "tp").astype(jnp.float32)
    back_one, grad_gain_one = rms_backward(grad_norm_in, normed_one, inv_one, first_gain)
    grad_rows = (grad_middle + back_one).astype(jnp.bfloat16).reshape(in_shape)
    scattered = (
        lax.psum_scatter(
            grad_win.astype(jnp.bfloat16), "fsdp", scatter_dimension=0, tiled=True
        ).astype(jnp.float32),
        lax.psum_scatter(
            grad_gu.astype(jnp.bfloat16), "fsdp", scatter_dimension=1, tiled=True
        ).astype(jnp.float32),
        lax.psum_scatter(
            grad_wout.astype(jnp.bfloat16), "fsdp", scatter_dimension=1, tiled=True
        ).astype(jnp.float32),
        lax.psum_scatter(
            grad_down.astype(jnp.bfloat16), "fsdp", scatter_dimension=1, tiled=True
        ).astype(jnp.float32),
    )
    summed = (
        lax.psum(scattered[0].astype(jnp.bfloat16), "ctx").astype(jnp.float32),
        lax.psum(scattered[1].astype(jnp.bfloat16), "ctx").astype(jnp.float32),
        lax.psum(scattered[2].astype(jnp.bfloat16), "ctx").astype(jnp.float32),
        lax.psum(scattered[3].astype(jnp.bfloat16), "ctx").astype(jnp.float32),
    )
    small_sums = lax.psum((grad_gain_one, grad_gain_two, grad_taps), ("fsdp", "ctx"))
    return (
        result,
        grad_rows,
        small_sums[0],
        summed[0],
        small_sums[2],
        summed[2],
        small_sums[1],
        summed[1],
        summed[3],
    )


def solution(mesh):
    placed = (
        P("fsdp", "ctx", None),
        P(),
        P("fsdp", None, "tp"),
        P(None, "tp"),
        P("tp", "fsdp"),
        P(),
        P(None, "fsdp", "tp"),
        P("tp", "fsdp"),
        P("fsdp", "ctx", None),
    )
    return jax.shard_map(
        body,
        mesh=mesh,
        in_specs=placed,
        out_specs=(
            P("fsdp", "ctx", None),
            P("fsdp", "ctx", None),
            P(),
            P("fsdp", None, "tp"),
            P(None, "tp"),
            P("tp", "fsdp"),
            P(),
            P(None, "fsdp", "tp"),
            P("tp", "fsdp"),
        ),
        check_vma=False,
    )
```

profile of v0, /device:TPU:0, one launch (start us, length us, event | category | flops | bytes accessed | tf_op | source)
XLA Modules:
  0.0 981.3 jit_solution(14446324722401698871)
XLA Ops:
  8.7 1.8 fusion.23
  10.4 27.0 %all_gather.17 = bf16[256,1024]{0,1:T(8,128)(2,1)S(1)} all-gather(bf16[256,64]{0,1:T(8,128)(2,1)} %param.13), channel_id=1, replica_groups=mesh['fsdp'=16,'ctx'=2,'tp'=4] {'fsdp'}, dimensions={1}, use_global_device_ids=true | all-gather | bytes 557056 | tf_op jit(solution)/shard_map/all_gather | solution.py:50
  37.5 22.4 %all-gather.4.cloned.1.call-done = bf16[1024,3,256]{2,0,1:T(8,128)(2,1)} async-done(((bf16[64,3,256]{2,0,1:T(8,128)(2,1)}), bf16[1024,3,256]{2,0,1:T(8,128)(2,1)}) %all-gather.4.cloned.1.call-update) | async-done | bytes 1572880 | tf_op jit(solution)/shard_map/all_gather | solution.py:48
  59.9 2.6 copy.25
  62.5 2.8 fusion.39
  65.4 2.6 collective-permute-start
  68.0 1.2 collective-permute-done
  69.4 1.2 multiply_convert_fusion.5
  70.5 2.3 fusion.79
  74.2 74.7 %all-reduce.13.cloned.1.call-done = f32[768,1024]{1,0:T(8,128)} async-done(((f32[768,1024]{1,0:T(8,128)}), f32[768,1024]{1,0:T(8,128)}) %all-reduce.13.cloned.1.call-update) | async-done | bytes 3145744 | tf_op jit(solution)/shard_map/psum | solution.py:72
  148.9 2.8 multiply_reduce_fusion.2
  151.8 57.5 %all-gather.6.cloned.1.call-done = bf16[2,1024,1152]{2,1,0:T(8,128)(2,1)} async-done(((bf16[2,64,1152]{2,1,0:T(8,128)(2,1)}), bf16[2,1024,1152]{2,1,0:T(8,128)(2,1)}) %all-gather.6.cloned.1.call-update) | async-done | bytes 4718608 | tf_op jit(solution)/shard_map/all_gather | solution.py:49
  209.3 8.3 fusion.66
  217.6 42.1 %all-gather.8.cloned.1.call-done = bf16[1152,1024]{0,1:T(8,128)(2,1)} async-done(((bf16[1152,64]{0,1:T(8,128)(2,1)}), bf16[1152,1024]{0,1:T(8,128)(2,1)}) %all-gather.8.cloned.1.call-update) | async-done | bytes 2359312 | tf_op jit(solution)/shard_map/all_gather | solution.py:51
  259.7 7.3 fusion.32
  267.0 1.2 copy-done.33
  268.8 5.5 fusion.27
  274.6 7.8 fusion
  282.4 12.7 %copy.28 = bf16[2,1024,1152]{2,0,1:T(2,128)(2,1)} copy(bf16[2,1024,1152]{1,2,0:T(8,128)(2,1)} %fusion) | data formatting | bytes 9437184 | tf_op jit(solution)/shard_map/convert_element_type | solution.py:146
  295.2 7.4 convolution_convert_fusion.1
  302.7 46.2 %all-reduce.15.cloned.1.call-done = f32[768,1024]{1,0:T(8,128)} async-done(((f32[768,1024]{1,0:T(8,128)}), f32[768,1024]{1,0:T(8,128)}) %all-reduce.15.cloned.1.call-update) | async-done | bytes 3145744 | tf_op jit(solution)/shard_map/psum | solution.py:105
  348.8 3.5 multiply_reduce_fusion
  352.3 0.8 multiply_add_fusion
  354.0 1.1 copy-done.3
  355.1 1.3 copy-done.9
  356.6 0.9 multiply_reduce_fusion.5
  357.8 1.4 collective-permute-start.1
  359.2 4.2 collective-permute-done.1
  364.5 2.7 convolution_convert_fusion.2
  367.3 3.5 convolution_convert_fusion.3
  370.8 1.2 dynamic-slice
  372.7 130.6 %all-reduce.17.cloned.1.call-done = bf16[2,1024,1152]{2,0,1:T(2,128)(2,1)} async-done(((bf16[2,1024,1152]{2,0,1:T(2,128)(2,1)}), bf16[2,1024,1152]{2,0,1:T(2,128)(2,1)}) %all-reduce.17.cloned.1.call-update) | async-done | bytes 4718608
  503.3 1.9 constant_dynamic-slice_fusion
  505.2 74.9 %reduce-scatter.8.cloned.1.call-done = bf16[1152,64]{0,1:T(8,128)(2,1)} async-done(((bf16[1152,1024]{0,1:T(8,128)(2,1)}), bf16[1152,64]{0,1:T(8,128)(2,1)}) %reduce-scatter.8.cloned.1.call-update) | async-done | bytes 147472 | tf_op jit(solution)/shard_map/reduce_scatter | solution.py:151
  580.1 72.2 %reduce-scatter.4.cloned.1.call-done = bf16[64,3,256]{2,0,1:T(8,128)(2,1)} async-done(((bf16[1024,3,256]{2,0,1:T(8,128)(2,1)}), bf16[64,3,256]{2,0,1:T(8,128)(2,1)}) %reduce-scatter.4.cloned.1.call-update) | async-done | bytes 98320 | tf_op jit(solution)/shard_map/reduce_scatter | solution.py:142
  652.6 7.3 fusion.33
  659.9 2.6 bitcast_convert_fusion
  663.1 57.8 %reduce-scatter.6.cloned.1.call-done = bf16[256,64]{0,1:T(8,128)(2,1)} async-done(((bf16[256,1024]{0,1:T(8,128)(2,1)}), bf16[256,64]{0,1:T(8,128)(2,1)}) %reduce-scatter.6.cloned.1.call-update) | async-done | bytes 32784 | tf_op jit(solution)/shard_map/reduce_scatter | solution.py:148
  721.0 8.3 psum.84
  729.9 29.4 %all-reduce.21.cloned.1.call-done = (bf16[2,64,1152]{2,0,1:T(2,128)(2,1)}, bf16[64,3,256]{2,0,1:T(8,128)(2,1)}, bf16[1152,64]{0,1:T(8,128)(2,1)}) async-done(((bf16[2,64,1152]{2,0,1:T(2,128)(2,1)}, bf16[64,3,256]{2,0,1:T(8,128)(2,1)}, bf16[1152,64]{0,1:T(8,128)(2,1)}), (bf16[2,64,1152]{2,0,1:T(2,128)(2,1)}, bf16[64,3,256]{2,0,1:T(8,128)(2,1)}, bf16[1152,64]{0,1:T(8,128)(2,1)})) %all-reduce.21.cloned.1.call-update) | async-done | bytes 540688 | tf_op jit(solution)/shard_map/psum | solution.py:157
  759.3 1.6 convert_element_type.145
  760.9 1.8 copy.29
  762.7 1.6 convert_element_type.154
  764.4 74.8 %all-reduce.19.cloned.1.call-done = (bf16[768,1024]{1,0:T(8,128)(2,1)}, bf16[768,1024]{1,0:T(8,128)(2,1)}) async-done(((bf16[768,1024]{1,0:T(8,128)(2,1)}, bf16[768,1024]{1,0:T(8,128)(2,1)}), (bf16[768,1024]{1,0:T(8,128)(2,1)}, bf16[768,1024]{1,0:T(8,128)(2,1)})) %all-reduce.19.cloned.1.call-update) | async-done | bytes 3145744 | tf_op jit(solution)/shard_map/psum | solution.py:83
  839.2 3.3 fusion.37
  842.5 1.2 fusion.21
  844.4 2.1 fusion.43
  846.4 128.3 %all-reduce.4 = (f32[1024]{0:T(1024)}, f32[3,256]{1,0:T(4,128)}, f32[1024]{0:T(1024)}) all-reduce(f32[1024]{0:T(1024)S(1)} %get-tuple-element.38, f32[3,256]{1,0:T(4,128)S(1)} %pad_maximum_fusion.10, f32[1024]{0:T(1024)S(1)} %copy-done.22), channel_id=1, replica_groups=mesh['fsdp'=16,'ctx'=2,'tp'=4] {'fsdp','ctx'}, use_global_device_ids=true, to_apply=%region_9.0 | all-reduce | flops 2816 | bytes 22528 | tf_op jit(solution)/shard_map/psum | solution.py:161
  (106 shorter events, 8.8 us)
Async XLA Ops:
  7.2 55.3 %copy-start.4 = (bf16[1,768,1024]{2,1,0:T(8,128)(2,1)S(1)}, bf16[1,768,1024]{2,1,0:T(8,128)(2,1)}, u32[]{:S(2)}) copy-start(bf16[1,768,1024]{2,1,0:T(8,128)(2,1)} %param.9) | copy-start | bytes 4718596
  7.2 52.7 %all-gather.4.cloned.1.call-start = ((), (), s32[]{:S(2)}) async-start(), calls=%async_computation.3 | async-start | bytes 1671168 | tf_op jit(solution)/shard_map/all_gather | solution.py:48
  7.9 141.0 %all-reduce.13.cloned.1.call-start = ((), (), s32[]{:S(2)}) async-start(), calls=%async_computation.4 | async-start | bytes 6291456 | tf_op jit(solution)/shard_map/psum | solution.py:72
  37.5 33.0 %copy-start.11 = (bf16[256,1024]{0,1:T(8,128)(2,1)}, bf16[256,1024]{0,1:T(8,128)(2,1)S(1)}, u32[]{:S(2)}) copy-start(bf16[256,1024]{0,1:T(8,128)(2,1)S(1)} %all_gather.17) | copy-start | bytes 1572868
  62.5 5.5 copy-start.29
  65.3 5.2 copy-start.8
  65.4 3.9 collective-permute-start
  68.0 4.8 copy-start.23
  68.0 4.8 copy-start.25
  68.0 4.8 copy-start.27
  69.4 3.5 copy-start.2
  70.5 3.7 copy-start.31
  72.9 136.4 %all-gather.6.cloned.1.call-start = ((), (), s32[]{:S(2)}) async-start(), calls=%async_computation.5 | async-start | bytes 5013504 | tf_op jit(solution)/shard_map/all_gather | solution.py:49
  73.6 186.1 %all-gather.8.cloned.1.call-start = ((), (), s32[]{:S(2)}) async-start(), calls=%async_computation.6 | async-start | bytes 2506752 | tf_op jit(solution)/shard_map/all_gather | solution.py:51
  74.2 274.6 %all-reduce.15.cloned.1.call-start = ((), (), s32[]{:S(2)}) async-start(), calls=%async_computation.7 | async-start | bytes 6291456 | tf_op jit(solution)/shard_map/psum | solution.py:105
  259.7 9.1 copy-start.32
  267.0 1.2 copy-start.33
  267.0 1.8 copy-start.34
  274.4 228.9 %all-reduce.17.cloned.1.call-start = ((), (), s32[]{:S(2)}) async-start(), calls=%async_computation.11 | async-start | bytes 9437184
  295.1 285.0 %reduce-scatter.8.cloned.1.call-start = ((), (), s32[]{:S(2)}) async-start(), calls=%async_computation.10 | async-start | bytes 2506752 | tf_op jit(solution)/shard_map/reduce_scatter | solution.py:151
  302.6 349.6 %reduce-scatter.4.cloned.1.call-start = ((), (), s32[]{:S(2)}) async-start(), calls=%async_computation.8 | async-start | bytes 1671168 | tf_op jit(solution)/shard_map/reduce_scatter | solution.py:142
  348.8 3.5 copy-start.7
  348.8 3.5 copy-start.15
  352.3 1.0 copy-start.12
  353.3 4.1 copy-start
  353.3 1.7 copy-start.3
  353.4 3.0 copy-start.9
  353.4 3.2 copy-start.13
  353.9 3.5 copy-start.24
  354.0 3.5 copy-start.26
  354.0 3.5 copy-start.28
  357.5 6.2 copy-start.16
  357.5 7.0 copy-start.5
  357.8 5.6 collective-permute-start.1
  363.6 0.8 copy-start.18
  363.6 0.9 copy-start.20
  367.2 353.7 %reduce-scatter.6.cloned.1.call-start = ((), (), s32[]{:S(2)}) async-start(), calls=%async_computation.9 | async-start | bytes 557056 | tf_op jit(solution)/shard_map/reduce_scatter | solution.py:148
  370.8 388.6 %all-reduce.21.cloned.1.call-start = ((), (), s32[]{:S(2)}) async-start(), calls=%async_computation.13 | async-start | bytes 1081344 | tf_op jit(solution)/shard_map/psum | solution.py:157
  652.3 7.6 copy-start.17
  652.3 186.9 %all-reduce.19.cloned.1.call-start = ((), (), s32[]{:S(2)}) async-start(), calls=%async_computation.12 | async-start | bytes 6291456 | tf_op jit(solution)/shard_map/psum | solution.py:83
  652.6 7.3 copy-start.14
  652.6 7.3 copy-start.19
  652.6 7.3 copy-start.21
  662.4 0.7 copy-start.30
  839.2 3.3 copy-start.6
  839.2 3.3 copy-start.10
  842.5 1.9 copy-start.1
  844.4 2.1 copy-start.22
Sparse Core Ops, SparseCore 0:
  10.5 49.3 all-gather.3
  73.0 75.8 all-reduce.12
  151.4 57.8 all-gather.5
  211.6 48.1 all-gather.7
  274.5 74.2 all-reduce.14
  351.2 152.0 all-reduce.16
  507.3 72.7 reduce-scatter.7
  584.5 67.6 reduce-scatter.3
  656.6 64.3 reduce-scatter.5
  724.2 35.0 all-reduce.20
  762.3 76.8 all-reduce.18
where the time goes:
time: 982 us; the launch traced here: 981 us
  waiting for transfers between devices  690 us (70%)
  blocking collectives  164 us (17%)
  matrix products  58.1 us (6%)
  local copies, waits for them, and re-layouts  27.1 us (3%)
  other arithmetic  22.7 us (2%)
  between operations  14.9 us (2%)
    unnamed x12, waiting for transfers between devices  133 us
    psum x1, blocking collectives, body(): lax.psum((grad_gain_one, grad_gain_two, grad_taps), ('fsdp', 'ctx'))  128 us
    reduce_scatter x1, waiting for transfers between devices, body(): lax.psum_scatter(grad_down.astype(jnp.bfloat16), 'fsdp', scatter_dimensio...  74.9 us
    psum x1, waiting for transfers between devices, body(): lax.psum(ffn_part.astype(jnp.bfloat16), 'tp').astype(jnp.float32)  74.8 us
    psum x1, waiting for transfers between devices, body(): middle = token_rows + lax.psum(mixer_part, 'tp')  74.7 us
    reduce_scatter x1, waiting for transfers between devices, body(): lax.psum_scatter(grad_win.astype(jnp.bfloat16), 'fsdp', scatter_dimension...  72.2 us
    reduce_scatter x1, waiting for transfers between devices, body(): lax.psum_scatter(grad_wout.astype(jnp.bfloat16), 'fsdp', scatter_dimensio...  57.8 us
    all_gather x1, waiting for transfers between devices, body(): lax.all_gather(gate_up_weight, 'fsdp', axis=1, tiled=True)  57.5 us
  transfers between devices with their start and end apart: 13, of which 13 were waited for; matrix products, arithmetic and copies ran while one was open for 7% of the time, Pallas kernels for 0%

commit v1 on v0

v1 whole, which is shorter than its diff:
```python
import jax
import jax.numpy as jnp
from jax import lax
from jax.sharding import PartitionSpec as P

EPSILON = 1e-05
BF = jnp.bfloat16
F32 = jnp.float32
NX, NY = 4, 4
ROWS = 192


def x_shift(v, d):
    return lax.ppermute(v, "tp", [(i, (i + d) % NX) for i in range(NX)])


def y_shift(v, d):
    route = []
    for f in range(16):
        zh, y, c = f // 8, (f // 2) % 4, f % 2
        route.append((f, zh * 8 + ((y + d) % NY) * 2 + c))
    return lax.ppermute(v, "fsdp", route)


def core_swap(v):
    return lax.ppermute(v, "fsdp", [(f, f ^ 1) for f in range(16)])


def z_cross(v):
    route = []
    for f in range(16):
        for c in range(2):
            route.append((f * 2 + c, (f ^ 8) * 2 + (c ^ 1)))
    return lax.ppermute(v, ("fsdp", "ctx"), route)


def ctx_swap(v):
    return lax.ppermute(v, "ctx", [(0, 1), (1, 0)])


def passed_along(block, distance):
    route = [(0, 1)] if distance == 1 else [(1, 0)]
    return lax.ppermute(block, "ctx", route)


def dot(a, b, dims=(((1,), (0,)), ((), ()))):
    return lax.dot_general(a, b, dims, preferred_element_type=F32)


CC = (((1,), (1,)), ((), ()))
RR = (((0,), (0,)), ((), ()))


def inv_rms_of(v):
    return lax.rsqrt(jnp.mean(v * v, axis=-1, keepdims=True) + EPSILON)


def place(pieces, spots, axis=0):
    size = pieces[0].shape[axis]
    shape = list(pieces[0].shape)
    shape[axis] = size * len(pieces)
    out = jnp.zeros(shape, pieces[0].dtype)
    for piece, spot in zip(pieces, spots):
        out = lax.dynamic_update_slice_in_dim(out, piece, spot * size, axis)
    return out


def block(v, spot, size=ROWS, axis=0):
    return lax.dynamic_slice_in_dim(v, spot * size, size, axis)


def gather_x(v):
    return [v, x_shift(v, 1), x_shift(v, -1), x_shift(v, 2)]


def scatter_x(parts):
    got = [
        x_shift(parts[3].astype(BF), 2),
        x_shift(parts[1].astype(BF), -1),
        x_shift(parts[2].astype(BF), 1),
    ]
    return parts[0] + got[0].astype(F32) + got[1].astype(F32) + got[2].astype(F32)


def body(
    tokens,
    norm_gain,
    in_weight,
    conv_weight,
    out_weight,
    ffn_gain,
    gate_up_weight,
    down_weight,
    cotangent,
):
    in_shape = tokens.shape
    width = in_shape[-1]
    tok = tokens.reshape(-1, width)
    cot = cotangent.reshape(-1, width)
    rows = tok.shape[0]
    fi = lax.axis_index("fsdp")
    zh, y, core = fi // 8, (fi // 2) % 4, fi % 2
    x = lax.axis_index("tp")
    spots = [x, (x + 3) % 4, (x + 1) % 4, (x + 2) % 4]
    gain1 = norm_gain.astype(F32)
    gain2 = ffn_gain.astype(F32)
    taps = conv_weight.astype(F32)

    packed_ffn = jnp.concatenate([gate_up_weight, down_weight.T[None]], 0)
    w_ffn = lax.all_gather(packed_ffn, "fsdp", axis=1, tiled=True)

    mine = jnp.concatenate([in_weight.reshape(64, 768), out_weight.T], 1)
    other = z_cross(mine)
    pair = place([mine[None], other[None]], [zh, 1 - zh])
    ys = [pair, y_shift(pair, 1), y_shift(pair, -1), y_shift(pair, 2)]
    col = place([v[:, None] for v in ys], [y, (y + 3) % 4, (y + 1) % 4, (y + 2) % 4], 1)
    col2 = core_swap(col)
    w_mix = place([col[:, :, None], col2[:, :, None]], [core, 1 - core], 2).reshape(width, 1024)
    w_in = w_mix[:, :768]
    w_out_t = w_mix[:, 768:]

    x32 = tok.astype(F32)
    inv1 = inv_rms_of(x32)
    normed1 = x32 * inv1
    normed_in = (normed1 * gain1).astype(BF)
    projected = dot(normed_in, w_in)
    gate_b, gate_c, values_v = projected[:, :256], projected[:, 256:512], projected[:, 512:]
    mixed_in = (gate_b * values_v).astype(BF)
    arrived = passed_along(mixed_in[rows - 2 :], 1)
    extended = jnp.concatenate([arrived, mixed_in], 0).astype(F32)
    conv_out = (
        taps[0] * extended[:rows] + taps[1] * extended[1 : rows + 1] + taps[2] * extended[2:]
    )
    gated = (gate_c * conv_out).astype(BF)
    mixer_part = dot(gated, w_out_t, CC)
    own_tok = block(tok, x).astype(F32)
    middle = own_tok + scatter_x([block(mixer_part, s) for s in spots])

    inv2 = inv_rms_of(middle)
    normed2 = middle * inv2
    nm = gather_x((normed2 * gain2).astype(BF))
    cots = [block(cot, s) for s in spots]
    w_g, w_u, w_dt = w_ffn[0], w_ffn[1], w_ffn[2]
    acts, ggs, gus, ffns, mids = [], [], [], [], []
    for piece, ct in zip(nm, cots):
        gate_g = dot(piece, w_g)
        up_u = dot(piece, w_u)
        sg = jax.nn.sigmoid(gate_g)
        silu = gate_g * sg
        act = (silu * up_u).astype(BF)
        grad_act = dot(ct, w_dt)
        gg = (grad_act * up_u * sg * (1.0 + gate_g * (1.0 - sg))).astype(BF)
        gu = (grad_act * silu).astype(BF)
        ffns.append(dot(act, w_dt, CC))
        mids.append(dot(gg, w_g, CC) + dot(gu, w_u, CC))
        acts.append(act)
        ggs.append(gg)
        gus.append(gu)
    ffns[0] = ffns[0] + middle
    out_part = place([f.astype(BF) for f in ffns], spots)
    result = lax.psum(out_part, "tp").reshape(in_shape)
    grad_mid_in = scatter_x(mids)
    nm_all = jnp.concatenate(nm, 0)
    cot_all = jnp.concatenate(cots, 0)
    act_all = jnp.concatenate(acts, 0)
    gg_all = jnp.concatenate(ggs, 0)
    gu_all = jnp.concatenate(gus, 0)
    g_ffn = jnp.stack(
        [dot(nm_all, gg_all, RR), dot(nm_all, gu_all, RR), dot(cot_all, act_all, RR)], 0
    ).astype(BF)

    cot_own = cots[0].astype(F32)
    sv = grad_mid_in * gain2
    grad_middle = cot_own + inv2 * (sv - normed2 * jnp.mean(sv * normed2, -1, keepdims=True))
    gain2_part = jnp.sum(grad_mid_in * normed2, 0)
    grad_branch = place(gather_x(grad_middle.astype(BF)), spots)

    grad_gated = dot(grad_branch, w_out_t)
    g_out_t = dot(grad_branch, gated, RR)
    grad_c = grad_gated * conv_out
    grad_conv = grad_gated * gate_c
    taps_part = jnp.stack(
        [
            jnp.sum(extended[:rows] * grad_conv, 0),
            jnp.sum(extended[1 : rows + 1] * grad_conv, 0),
            jnp.sum(extended[2:] * grad_conv, 0),
        ],
        0,
    )
    back = passed_along(grad_conv[:2], -1)
    padded = jnp.concatenate([grad_conv, back], 0)
    grad_mixed = taps[2] * padded[:rows] + taps[1] * padded[1 : rows + 1] + taps[0] * padded[2:]
    rounded = grad_mixed.astype(BF).astype(F32)
    grad_proj = jnp.concatenate([rounded * values_v, grad_c, rounded * gate_b], 1).astype(BF)
    norm_part = dot(grad_proj, w_in, CC)
    gain1_part = jnp.sum(norm_part * normed1, 0)
    grad_norm_in = scatter_x([block(norm_part, s) for s in spots])
    g_in = dot(normed_in, grad_proj, RR)
    g_mix = jnp.concatenate([g_in, g_out_t], 1).astype(BF)

    inv1_own = inv_rms_of(own_tok)
    normed1_own = own_tok * inv1_own
    su = grad_norm_in * gain1
    grad_rows = grad_middle + inv1_own * (
        su - normed1_own * jnp.mean(su * normed1_own, -1, keepdims=True)
    )
    input_grad = place(gather_x(grad_rows.astype(BF)), spots).reshape(in_shape)

    def reduce_grads(g):
        n, _, m = g.shape
        g = g.reshape(n, 2, 4, 2, 64, m)
        send = lax.dynamic_index_in_dim(g, 1 - core, 3, False)
        keep = lax.dynamic_index_in_dim(g, core, 3, False)
        h = (keep.astype(F32) + core_swap(send).astype(F32)).astype(BF)
        part = [lax.dynamic_index_in_dim(h, s, 2, False) for s in (y, (y + 3) % 4, (y + 1) % 4, (y + 2) % 4)]
        k = (
            part[0].astype(F32)
            + y_shift(part[1], -1).astype(F32)
            + y_shift(part[2], 1).astype(F32)
            + y_shift(part[3], 2).astype(F32)
        ).astype(BF)
        own = lax.dynamic_index_in_dim(k, zh, 1, False).astype(F32)
        far = lax.dynamic_index_in_dim(k, 1 - zh, 1, False)
        half = (own + z_cross(far).astype(F32)).astype(BF)
        return half.astype(F32) + ctx_swap(half).astype(F32)

    r_ffn = reduce_grads(g_ffn)
    r_mix = reduce_grads(g_mix[None])[0]

    small = jnp.concatenate([gain1_part, gain2_part, taps_part.reshape(-1)], 0).reshape(22, 128)
    small = small + core_swap(small)
    small = small + y_shift(small, 1) + y_shift(small, -1) + y_shift(small, 2)
    small = small + z_cross(small)
    small = small + ctx_swap(small)
    gains = small[:16]
    gains = gains + x_shift(gains, 1) + x_shift(gains, -1) + x_shift(gains, 2)
    return (
        result,
        input_grad,
        gains[:8].reshape(-1),
        r_mix[:, :768].reshape(64, 3, 256),
        small[16:].reshape(3, 256),
        r_mix[:, 768:].T,
        gains[8:].reshape(-1),
        r_ffn[:2],
        r_ffn[2].T,
    )


def solution(mesh):
    placed = (
        P("fsdp", "ctx", None),
        P(),
        P("fsdp", None, "tp"),
        P(None, "tp"),
        P("tp", "fsdp"),
        P(),
        P(None, "fsdp", "tp"),
        P("tp", "fsdp"),
        P("fsdp", "ctx", None),
    )
    return jax.shard_map(
        body,
        mesh=mesh,
        in_specs=placed,
        out_specs=(
            P("fsdp", "ctx", None),
            P("fsdp", "ctx", None),
            P(),
            P("fsdp", None, "tp"),
            P(None, "tp"),
            P("tp", "fsdp"),
            P(),
            P(None, "fsdp", "tp"),
            P("tp", "fsdp"),
        ),
        check_vma=False,
    )
```

time: 982 us -> 346 us (0.35)
  waiting for transfers between devices: 690 us -> 121 us
  blocking collectives: 164 us -> 0 us
  starting transfers between devices: 4.83 us -> 93.1 us
    psum x4 -> x1, waiting for transfers between devices: 225 us -> 0.01 us  [body(): result = lax.psum(out_part, 'tp').reshape(in_shape)]
    reduce_scatter x3 -> x0, waiting for transfers between devices: 205 us -> none  [the longest x1 74.9 us: body(): lax.psum_scatter(grad_down.astype(jnp.bfloat16), 'fsdp', scatter_dimensio...]
    psum x2 -> x0, blocking collectives: 137 us -> none  [the longest x1 128 us: body(): lax.psum((grad_gain_one, grad_gain_two, grad_taps), ('fsdp', 'ctx'))]
    unnamed x12 -> x2, waiting for transfers between devices: 133 us -> 0.03 us
    all_gather x3 -> x1, waiting for transfers between devices: 122 us -> 0.01 us  [body(): w_ffn = lax.all_gather(packed_ffn, 'fsdp', axis=1, tiled=True)]
    ppermute x2 -> x46, waiting for transfers between devices: 5.4 us -> 121 us  [the longest x21 50.3 us: x_shift(): return lax.ppermute(v, 'tp', [(i, (i + d) % NX) for i in range(NX)])]
    ppermute x2 -> x46, starting transfers between devices: 3.98 us -> 93.1 us  [the longest x21 59.3 us: x_shift(): return lax.ppermute(v, 'tp', [(i, (i + d) % NX) for i in range(NX)])]
    all_gather x1 -> x0, blocking collectives: 27 us -> none  [body(): lax.all_gather(out_weight, 'fsdp', axis=1, tiled=True)]
  transfers between devices with their start and end apart: 13 -> 48, of which waited for: 13 -> 20; matrix products, arithmetic and copies ran while one was open for 7% -> 30% of each run, Pallas kernels for 0% -> 0%
where the time goes in v1:
time: 346 us; the launch traced here: 343 us
  waiting for transfers between devices  121 us (35%)
  starting transfers between devices  93.1 us (27%)
  matrix products  55 us (16%)
  other arithmetic  29.9 us (9%)
  local copies, waits for them, and re-layouts  27.5 us (8%)
  between operations  15.7 us (5%)
    ppermute x21, starting transfers between devices, x_shift(): return lax.ppermute(v, 'tp', [(i, (i + d) % NX) for i in range(NX)])  59.3 us
    dot_general x33, matrix products, dot(): return lax.dot_general(a, b, dims, preferred_element_type=F32)  55 us
    ppermute x21, waiting for transfers between devices, x_shift(): return lax.ppermute(v, 'tp', [(i, (i + d) % NX) for i in range(NX)])  50.3 us
    ppermute x12, waiting for transfers between devices, y_shift(): return lax.ppermute(v, 'fsdp', route)  46.8 us
    ppermute x12, starting transfers between devices, y_shift(): return lax.ppermute(v, 'fsdp', route)  19 us
    ppermute x4, starting transfers between devices, z_cross(): return lax.ppermute(v, ('fsdp', 'ctx'), route)  9.86 us
    unnamed x130, local copies, waits for them, and re-layouts  9.64 us
    ppermute x4, waiting for transfers between devices, z_cross(): return lax.ppermute(v, ('fsdp', 'ctx'), route)  9.04 us
  transfers between devices with their start and end apart: 48, of which 20 were waited for; matrix products, arithmetic and copies ran while one was open for 30% of the time, Pallas kernels for 0%

profile of v1, /device:TPU:0, one launch (start us, length us, event | category | flops | bytes accessed | tf_op | source)
XLA Modules:
  0.0 342.8 jit_solution(1104661779309496877)
XLA Ops:
  11.0 4.2 %collective-permute-start = (bf16[64,1024]{1,0:T(8,128)(2,1)S(1)}, bf16[64,1024]{1,0:T(8,128)(2,1)S(1)}, u32[]{:S(2)}, u32[]{:S(2)}) collective-permute-start(bf16[64,1024]{1,0:T(8,128)(2,1)S(1)} %pad_maximum_fusion.9), channel_id=1, source_target_pairs={{0,68},{4,64},{8,76},{12,72},{16,84},{20,80},{24,92},{28,88},{32,1... | collective-permute-start | bytes 393224 | tf_op jit(solution)/shard_map/ppermute | solution.py:34
  16.0 2.7 collective-permute-done
  24.1 5.3 %collective-permute-done.1 = bf16[2,64,1024]{2,1,0:T(8,128)(2,1)S(1)} collective-permute-done((bf16[2,64,1024]{2,1,0:T(8,128)(2,1)S(1)}, bf16[2,64,1024]{2,1,0:T(8,128)(2,1)S(1)}, u32[]{:S(2)}, u32[]{:S(2)}) %collective-permute-start.1) | collective-permute-done | bytes 262176 | tf_op jit(solution)/shard_map/ppermute | solution.py:22
  29.5 5.0 %collective-permute-done.2 = bf16[2,64,1024]{2,1,0:T(8,128)(2,1)S(1)} collective-permute-done((bf16[2,64,1024]{2,1,0:T(8,128)(2,1)S(1)}, bf16[2,64,1024]{2,1,0:T(8,128)(2,1)S(1)}, u32[]{:S(2)}, u32[]{:S(2)}) %collective-permute-start.2) | collective-permute-done | bytes 262176 | tf_op jit(solution)/shard_map/ppermute | solution.py:22
  34.5 7.0 %collective-permute-done.3 = bf16[2,64,1024]{2,1,0:T(8,128)(2,1)S(1)} collective-permute-done((bf16[2,64,1024]{2,1,0:T(8,128)(2,1)S(1)}, bf16[2,64,1024]{2,1,0:T(8,128)(2,1)S(1)}, u32[]{:S(2)}, u32[]{:S(2)}) %collective-permute-start.3) | collective-permute-done | bytes 262176 | tf_op jit(solution)/shard_map/ppermute | solution.py:22
  51.3 2.6 multiply_convert_fusion.14
  63.9 6.5 %collective-permute-done.8 = bf16[192,1024]{1,0:T(8,128)(2,1)} collective-permute-done((bf16[192,1024]{1,0:T(8,128)(2,1)}, bf16[192,1024]{1,0:T(8,128)(2,1)}, u32[]{:S(2)}, u32[]{:S(2)}) %collective-permute-start.8) | collective-permute-done | bytes 393248 | tf_op jit(solution)/shard_map/ppermute | solution.py:14
  70.4 7.2 %collective-permute-done.7 = bf16[192,1024]{1,0:T(8,128)(2,1)} collective-permute-done((bf16[192,1024]{1,0:T(8,128)(2,1)}, bf16[192,1024]{1,0:T(8,128)(2,1)}, u32[]{:S(2)}, u32[]{:S(2)}) %collective-permute-start.7) | collective-permute-done | bytes 393248 | tf_op jit(solution)/shard_map/ppermute | solution.py:14
  83.5 2.1 collective-permute-start.10
  86.3 2.5 fusion.102
  88.8 12.2 %collective-permute-done.10 = bf16[192,1024]{1,0:T(8,128)(2,1)S(1)} collective-permute-done((bf16[192,1024]{1,0:T(8,128)(2,1)S(1)}, bf16[192,1024]{1,0:T(8,128)(2,1)S(1)}, u32[]{:S(2)}, u32[]{:S(2)}) %collective-permute-start.10) | collective-permute-done | bytes 393248 | tf_op jit(solution)/shard_map/ppermute | solution.py:14
  101.0 2.3 fusion.99
  106.3 13.0 %collective-permute-start.14 = (bf16[192,1024]{1,0:T(8,128)(2,1)S(1)}, bf16[192,1024]{1,0:T(8,128)(2,1)S(1)}, u32[]{:S(2)}, u32[]{:S(2)}) collective-permute-start(bf16[192,1024]{1,0:T(8,128)(2,1)S(1)} %fusion.46), channel_id=1, source_target_pairs={{0,1},{1,2},{2,3},{3,0},{4,5},{5,6},{6,7},{7,4},{8,9},{9,10},{10,1... | collective-permute-start | bytes 1179656 | tf_op jit(solution)/shard_map/ppermute | solution.py:14
  123.8 3.7 %collective-permute-start.13 = (bf16[192,1024]{1,0:T(8,128)(2,1)S(1)}, bf16[192,1024]{1,0:T(8,128)(2,1)S(1)}, u32[]{:S(2)}, u32[]{:S(2)}) collective-permute-start(bf16[192,1024]{1,0:T(8,128)(2,1)S(1)} %fusion.45), channel_id=1, source_target_pairs={{0,3},{1,0},{2,1},{3,2},{4,7},{5,4},{6,5},{7,6},{8,11},{9,8},{10,9... | collective-permute-start | bytes 1179656 | tf_op jit(solution)/shard_map/ppermute | solution.py:14
  136.0 2.3 convolution_convert_fusion
  138.2 2.3 convolution_convert_fusion.1
  140.5 2.3 convolution_convert_fusion.2
  146.5 2.8 fusion.93
  149.3 3.7 %multiply_reduce_fusion.3 = (f32[1024]{0:T(1024)}, f32[192]{0:T(256)S(1)}, f32[192,1024]{1,0:T(8,128)S(1)}) fusion(f32[192,1024]{1,0:T(8,128)S(1)} %copy-done.1, f32[192]{0:T(256)S(1)} %add_rsqrt_fusion.2, f32[1024]{0:T(1024)S(1)} %convert_element_type.300, bf16[192,1024]{1,0:T(8,128)(2,1)S(1)} %collective-permute-done.14, ...), kind=kOutput, calls=%fused_computation.145 | convolution fusion | flops 455539520 | bytes 6350336 | tf_op jit(solution)/shard_map/dot_general | solution.py:47
  162.8 12.3 %collective-permute-done.15 = bf16[192,1024]{1,0:T(8,128)(2,1)S(1)} collective-permute-done((bf16[192,1024]{1,0:T(8,128)(2,1)S(1)}, bf16[192,1024]{1,0:T(8,128)(2,1)S(1)}, u32[]{:S(2)}, u32[]{:S(2)}) %collective-permute-start.15) | collective-permute-done | bytes 393248 | tf_op jit(solution)/shard_map/ppermute | solution.py:14
  175.2 2.3 collective-permute-done.16
  177.7 3.4 multiply_reduce_fusion.2
  183.9 4.4 %collective-permute-done.18 = f32[2,256]{1,0:T(2,128)} collective-permute-done((f32[2,256]{1,0:T(2,128)}, f32[2,256]{1,0:T(2,128)}, u32[]{:S(2)}, u32[]{:S(2)}) %collective-permute-start.18) | collective-permute-done | bytes 2080 | tf_op jit(solution)/shard_map/ppermute | solution.py:43
  188.3 2.5 fusion.77
  194.5 2.1 fusion.88
  196.7 3.5 %fusion.52 = bf16[1,768,1024]{2,1,0:T(8,128)(2,1)} fusion(bf16[1,768,1024]{2,1,0:T(8,128)(2,1)} %fusion.50, s32[]{:T(128)S(6)} %select_n.154, bf16[192,1152]{1,0:T(8,128)(2,1)S(1)} %copy-done.59, bf16[3,1024,1152]{2,1,0:T(8,128)(2,1)} %all-gather.2.cloned.1.call-done), kind=kOutput, calls=%fused_computation.81 | convolution fusion | flops 453181440 | bytes 3194884 | tf_op jit(solution)/shard_map/dot_general | solution.py:47
  200.3 3.5 %collective-permute-start.27 = (f32[22,128]{1,0:T(8,128)S(1)}, f32[22,128]{1,0:T(8,128)S(1)}, u32[]{:S(2)}, u32[]{:S(2)}) collective-permute-start(f32[22,128]{1,0:T(8,128)S(1)} %fusion.112), channel_id=1, source_target_pairs={{0,48},{8,56},{16,0},{24,8},{32,16},{40,24},{48,32},{56,40},{64,11... | collective-permute-start | bytes 33800 | tf_op jit(solution)/shard_map/ppermute | solution.py:22
  205.5 3.2 collective-permute-done.26
  209.3 2.3 collective-permute-start.29
  214.2 2.6 copy.38
  219.3 3.2 fusion.38
  222.5 3.7 %collective-permute-start.33 = (f32[16,128]{1,0:T(8,128)S(1)}, f32[16,128]{1,0:T(8,128)}, u32[]{:S(2)}, u32[]{:S(2)}) collective-permute-start(f32[16,128]{1,0:T(8,128)S(1)} %slice.128), channel_id=1, source_target_pairs={{0,2},{1,3},{2,0},{3,1},{4,6},{5,7},{6,4},{7,5},{8,10},{9,11},{10,... | collective-permute-start | bytes 24584 | tf_op jit(solution)/shard_map/ppermute | solution.py:14
  226.2 2.0 collective-permute-start.31
  231.6 3.4 fusion.54
  237.8 4.3 %collective-permute-done.20 = bf16[192,1024]{1,0:T(8,128)(2,1)} collective-permute-done((bf16[192,1024]{1,0:T(8,128)(2,1)}, bf16[192,1024]{1,0:T(8,128)(2,1)}, u32[]{:S(2)}, u32[]{:S(2)}) %collective-permute-start.20) | collective-permute-done | bytes 393248 | tf_op jit(solution)/shard_map/ppermute | solution.py:14
  244.4 2.4 bitcast_dynamic-update-slice_fusion.5
  246.8 14.0 %collective-permute-start.22 = (bf16[192,1024]{1,0:T(8,128)(2,1)S(1)}, bf16[192,1024]{1,0:T(8,128)(2,1)S(1)}, u32[]{:S(2)}, u32[]{:S(2)}) collective-permute-start(bf16[192,1024]{1,0:T(8,128)(2,1)S(1)} %get-tuple-element.43), channel_id=1, source_target_pairs={{0,1},{1,2},{2,3},{3,0},{4,5},{5,6},{6,7},{7,4},{8,9},{9,10},{10,1... | collective-permute-start | bytes 1179656 | tf_op jit(solution)/shard_map/ppermute | solution.py:14
  260.8 3.2 collective-permute-start.23
  265.8 3.2 fusion
  269.3 3.6 %collective-permute-start.43 = (bf16[3,2,64,1152]{3,2,0,1:T(8,128)(2,1)S(1)}, bf16[3,2,64,1152]{3,2,0,1:T(8,128)(2,1)S(1)}, u32[]{:S(2)}, u32[]{:S(2)}) collective-permute-start(bf16[3,2,64,1152]{3,2,0,1:T(8,128)(2,1)S(1)} %get-tuple-element.55), channel_id=1, source_target_pairs={{0,32},{8,40},{16,48},{24,56},{32,0},{40,8},{48,16},{56,24},{64,96... | collective-permute-start | bytes 2654216 | tf_op jit(solution)/shard_map/ppermute | solution.py:22
  272.9 3.2 collective-permute-start.41
  276.7 3.2 collective-permute-start.35
  280.1 26.1 %collective-permute-done.36 = bf16[1,2,64,1024]{3,2,1,0:T(8,128)(2,1)S(1)} collective-permute-done((bf16[1,2,64,1024]{3,2,1,0:T(8,128)(2,1)S(1)}, bf16[1,2,64,1024]{3,2,1,0:T(8,128)(2,1)S(1)}, u32[]{:S(2)}, u32[]{:S(2)}) %collective-permute-start.36) | collective-permute-done | bytes 262176 | tf_op jit(solution)/shard_map/ppermute | solution.py:22
  308.7 2.9 collective-permute-start.44
  311.7 3.7 %collective-permute-done.24 = bf16[192,1024]{1,0:T(8,128)(2,1)S(1)} collective-permute-done((bf16[192,1024]{1,0:T(8,128)(2,1)S(1)}, bf16[192,1024]{1,0:T(8,128)(2,1)S(1)}, u32[]{:S(2)}, u32[]{:S(2)}) %collective-permute-start.24) | collective-permute-done | bytes 393248 | tf_op jit(solution)/shard_map/ppermute | solution.py:14
  315.6 6.3 %collective-permute-done.44 = bf16[3,64,1152]{2,1,0:T(8,128)(2,1)S(1)} collective-permute-done((bf16[3,64,1152]{2,1,0:T(8,128)(2,1)S(1)}, bf16[3,64,1152]{2,1,0:T(8,128)(2,1)S(1)}, u32[]{:S(2)}, u32[]{:S(2)}) %collective-permute-start.44) | collective-permute-done | bytes 442400 | tf_op jit(solution)/shard_map/ppermute | solution.py:34
  323.6 7.8 %collective-permute-done.45 = bf16[3,64,1152]{2,1,0:T(8,128)(2,1)S(1)} collective-permute-done((bf16[3,64,1152]{2,1,0:T(8,128)(2,1)S(1)}, bf16[3,64,1152]{2,1,0:T(8,128)(2,1)S(1)}, u32[]{:S(2)}, u32[]{:S(2)}) %collective-permute-start.45) | collective-permute-done | bytes 442400 | tf_op jit(solution)/shard_map/ppermute | solution.py:38
  333.1 2.7 copy.77
  (295 shorter events, 96.3 us)
Async XLA Ops:
  7.2 79.2 %all-gather.2.cloned.1.call-start = ((), (), s32[]{:S(2)}) async-start(), calls=%async_computation | async-start | bytes 7520256 | tf_op jit(solution)/shard_map/all_gather | solution.py:110
  9.1 323.9 %all-reduce.2.cloned.1.call-start = ((), (), s32[]{:S(2)}) async-start(), calls=%async_computation.1 | async-start | bytes 3145728 | tf_op jit(solution)/shard_map/psum | solution.py:161
  11.0 7.7 %collective-permute-start = (bf16[64,1024]{1,0:T(8,128)(2,1)S(1)}, bf16[64,1024]{1,0:T(8,128)(2,1)S(1)}, u32[]{:S(2)}, u32[]{:S(2)}) collective-permute-start(bf16[64,1024]{1,0:T(8,128)(2,1)S(1)} %pad_maximum_fusion.9), channel_id=1, source_target_pairs={{0,68},{4,64},{8,76},{12,72},{16,84},{20,80},{24,92},{28,88},{32,1... | collective-permute-start | bytes 393224 | tf_op jit(solution)/shard_map/ppermute | solution.py:34
  18.7 10.8 %collective-permute-start.1 = (bf16[2,64,1024]{2,1,0:T(8,128)(2,1)S(1)}, bf16[2,64,1024]{2,1,0:T(8,128)(2,1)S(1)}, u32[]{:S(2)}, u32[]{:S(2)}) collective-permute-start(bf16[2,64,1024]{2,1,0:T(8,128)(2,1)S(1)} %bitcast_dynamic-update-slice_fusion.10), channel_id=1, source_target_pairs={{0,16},{8,24},{16,32},{24,40},{32,48},{40,56},{48,0},{56,8},{64,80... | collective-permute-start | bytes 786440 | tf_op jit(solution)/shard_map/ppermute | solution.py:22
  20.3 14.1 %collective-permute-start.2 = (bf16[2,64,1024]{2,1,0:T(8,128)(2,1)S(1)}, bf16[2,64,1024]{2,1,0:T(8,128)(2,1)S(1)}, u32[]{:S(2)}, u32[]{:S(2)}) collective-permute-start(bf16[2,64,1024]{2,1,0:T(8,128)(2,1)S(1)} %bitcast_dynamic-update-slice_fusion.10), channel_id=1, source_target_pairs={{0,48},{8,56},{16,0},{24,8},{32,16},{40,24},{48,32},{56,40},{64,11... | collective-permute-start | bytes 786440 | tf_op jit(solution)/shard_map/ppermute | solution.py:22
  22.0 19.4 %collective-permute-start.3 = (bf16[2,64,1024]{2,1,0:T(8,128)(2,1)S(1)}, bf16[2,64,1024]{2,1,0:T(8,128)(2,1)S(1)}, u32[]{:S(2)}, u32[]{:S(2)}) collective-permute-start(bf16[2,64,1024]{2,1,0:T(8,128)(2,1)S(1)} %bitcast_dynamic-update-slice_fusion.10), channel_id=1, source_target_pairs={{0,32},{8,40},{16,48},{24,56},{32,0},{40,8},{48,16},{56,24},{64,96... | collective-permute-start | bytes 786440 | tf_op jit(solution)/shard_map/ppermute | solution.py:22
  41.4 2.9 collective-permute-start.4
  48.6 2.6 collective-permute-start.5
  57.8 12.6 %collective-permute-start.8 = (bf16[192,1024]{1,0:T(8,128)(2,1)}, bf16[192,1024]{1,0:T(8,128)(2,1)}, u32[]{:S(2)}, u32[]{:S(2)}) collective-permute-start(bf16[192,1024]{1,0:T(8,128)(2,1)} %get-tuple-element.61), channel_id=1, source_target_pairs={{0,1},{1,2},{2,3},{3,0},{4,5},{5,6},{6,7},{7,4},{8,9},{9,10},{10,1... | collective-permute-start | bytes 1179656 | tf_op jit(solution)/shard_map/ppermute | solution.py:14
  59.3 18.3 %collective-permute-start.7 = (bf16[192,1024]{1,0:T(8,128)(2,1)}, bf16[192,1024]{1,0:T(8,128)(2,1)}, u32[]{:S(2)}, u32[]{:S(2)}) collective-permute-start(bf16[192,1024]{1,0:T(8,128)(2,1)} %get-tuple-element.62), channel_id=1, source_target_pairs={{0,3},{1,0},{2,1},{3,2},{4,7},{5,4},{6,5},{7,6},{8,11},{9,8},{10,9... | collective-permute-start | bytes 1179656 | tf_op jit(solution)/shard_map/ppermute | solution.py:14
  61.0 18.3 %collective-permute-start.6 = (bf16[192,1024]{1,0:T(8,128)(2,1)}, bf16[192,1024]{1,0:T(8,128)(2,1)}, u32[]{:S(2)}, u32[]{:S(2)}) collective-permute-start(bf16[192,1024]{1,0:T(8,128)(2,1)} %get-tuple-element.60), channel_id=1, source_target_pairs={{0,2},{1,3},{2,0},{3,1},{4,6},{5,7},{6,4},{7,5},{8,10},{9,11},{10,... | collective-permute-start | bytes 1179656 | tf_op jit(solution)/shard_map/ppermute | solution.py:14
  82.3 37.8 %collective-permute-start.9 = (bf16[192,1024]{1,0:T(8,128)(2,1)S(1)}, bf16[192,1024]{1,0:T(8,128)(2,1)S(1)}, u32[]{:S(2)}, u32[]{:S(2)}) collective-permute-start(bf16[192,1024]{1,0:T(8,128)(2,1)S(1)} %multiply_convert_fusion.13), channel_id=1, source_target_pairs={{0,1},{1,2},{2,3},{3,0},{4,5},{5,6},{6,7},{7,4},{8,9},{9,10},{10,1... | collective-permute-start | bytes 1179656 | tf_op jit(solution)/shard_map/ppermute | solution.py:14
  83.5 17.5 %collective-permute-start.10 = (bf16[192,1024]{1,0:T(8,128)(2,1)S(1)}, bf16[192,1024]{1,0:T(8,128)(2,1)S(1)}, u32[]{:S(2)}, u32[]{:S(2)}) collective-permute-start(bf16[192,1024]{1,0:T(8,128)(2,1)S(1)} %multiply_convert_fusion.13), channel_id=1, source_target_pairs={{0,3},{1,0},{2,1},{3,2},{4,7},{5,4},{6,5},{7,6},{8,11},{9,8},{10,9... | collective-permute-start | bytes 1179656 | tf_op jit(solution)/shard_map/ppermute | solution.py:14
  85.7 42.6 %collective-permute-start.11 = (bf16[192,1024]{1,0:T(8,128)(2,1)S(1)}, bf16[192,1024]{1,0:T(8,128)(2,1)S(1)}, u32[]{:S(2)}, u32[]{:S(2)}) collective-permute-start(bf16[192,1024]{1,0:T(8,128)(2,1)S(1)} %multiply_convert_fusion.13), channel_id=1, source_target_pairs={{0,2},{1,3},{2,0},{3,1},{4,6},{5,7},{6,4},{7,5},{8,10},{9,11},{10,... | collective-permute-start | bytes 1179656 | tf_op jit(solution)/shard_map/ppermute | solution.py:14
  106.3 42.9 %collective-permute-start.14 = (bf16[192,1024]{1,0:T(8,128)(2,1)S(1)}, bf16[192,1024]{1,0:T(8,128)(2,1)S(1)}, u32[]{:S(2)}, u32[]{:S(2)}) collective-permute-start(bf16[192,1024]{1,0:T(8,128)(2,1)S(1)} %fusion.46), channel_id=1, source_target_pairs={{0,1},{1,2},{2,3},{3,0},{4,5},{5,6},{6,7},{7,4},{8,9},{9,10},{10,1... | collective-permute-start | bytes 1179656 | tf_op jit(solution)/shard_map/ppermute | solution.py:14
  123.8 25.5 %collective-permute-start.13 = (bf16[192,1024]{1,0:T(8,128)(2,1)S(1)}, bf16[192,1024]{1,0:T(8,128)(2,1)S(1)}, u32[]{:S(2)}, u32[]{:S(2)}) collective-permute-start(bf16[192,1024]{1,0:T(8,128)(2,1)S(1)} %fusion.45), channel_id=1, source_target_pairs={{0,3},{1,0},{2,1},{3,2},{4,7},{5,4},{6,5},{7,6},{8,11},{9,8},{10,9... | collective-permute-start | bytes 1179656 | tf_op jit(solution)/shard_map/ppermute | solution.py:14
  131.9 17.4 %collective-permute-start.12 = (bf16[192,1024]{1,0:T(8,128)(2,1)S(1)}, bf16[192,1024]{1,0:T(8,128)(2,1)S(1)}, u32[]{:S(2)}, u32[]{:S(2)}) collective-permute-start(bf16[192,1024]{1,0:T(8,128)(2,1)S(1)} %fusion.44), channel_id=1, source_target_pairs={{0,2},{1,3},{2,0},{3,1},{4,6},{5,7},{6,4},{7,5},{8,10},{9,11},{10,... | collective-permute-start | bytes 1179656 | tf_op jit(solution)/shard_map/ppermute | solution.py:14
  146.5 119.3 %collective-permute-start.40 = (bf16[3,2,4,64,1152]{4,3,0,1,2:T(8,128)(2,1)}, bf16[3,2,4,64,1152]{4,3,0,1,2:T(8,128)(2,1)}, u32[]{:S(2)}, u32[]{:S(2)}) collective-permute-start(bf16[3,2,4,64,1152]{4,3,0,1,2:T(8,128)(2,1)} %bitcast.233), channel_id=1, source_target_pairs={{0,8},{8,0},{16,24},{24,16},{32,40},{40,32},{48,56},{56,48},{64,72... | collective-permute-start | bytes 10616840 | tf_op jit(solution)/shard_map/ppermute | solution.py:26
  153.5 21.6 %collective-permute-start.15 = (bf16[192,1024]{1,0:T(8,128)(2,1)S(1)}, bf16[192,1024]{1,0:T(8,128)(2,1)S(1)}, u32[]{:S(2)}, u32[]{:S(2)}) collective-permute-start(bf16[192,1024]{1,0:T(8,128)(2,1)S(1)} %get-tuple-element.47), channel_id=1, source_target_pairs={{0,1},{1,2},{2,3},{3,0},{4,5},{5,6},{6,7},{7,4},{8,9},{9,10},{10,1... | collective-permute-start | bytes 1179656 | tf_op jit(solution)/shard_map/ppermute | solution.py:14
  158.5 19.1 %collective-permute-start.16 = (bf16[192,1024]{1,0:T(8,128)(2,1)S(1)}, bf16[192,1024]{1,0:T(8,128)(2,1)S(1)}, u32[]{:S(2)}, u32[]{:S(2)}) collective-permute-start(bf16[192,1024]{1,0:T(8,128)(2,1)S(1)} %get-tuple-element.47), channel_id=1, source_target_pairs={{0,3},{1,0},{2,1},{3,2},{4,7},{5,4},{6,5},{7,6},{8,11},{9,8},{10,9... | collective-permute-start | bytes 1179656 | tf_op jit(solution)/shard_map/ppermute | solution.py:14
  160.3 17.3 %collective-permute-start.17 = (bf16[192,1024]{1,0:T(8,128)(2,1)S(1)}, bf16[192,1024]{1,0:T(8,128)(2,1)S(1)}, u32[]{:S(2)}, u32[]{:S(2)}) collective-permute-start(bf16[192,1024]{1,0:T(8,128)(2,1)S(1)} %get-tuple-element.47), channel_id=1, source_target_pairs={{0,2},{1,3},{2,0},{3,1},{4,6},{5,7},{6,4},{7,5},{8,10},{9,11},{10,... | collective-permute-start | bytes 1179656 | tf_op jit(solution)/shard_map/ppermute | solution.py:14
  182.5 5.8 %collective-permute-start.18 = (f32[2,256]{1,0:T(2,128)}, f32[2,256]{1,0:T(2,128)}, u32[]{:S(2)}, u32[]{:S(2)}) collective-permute-start(f32[2,256]{1,0:T(2,128)} %slice.125), channel_id=1, source_target_pairs={{4,0},{5,1},{6,2},{7,3},{12,8},{13,9},{14,10},{15,11},{20,16},{21,... | collective-permute-start | bytes 6152 | tf_op jit(solution)/shard_map/ppermute | solution.py:43
  196.6 3.6 %collective-permute-start.25 = (f32[22,128]{1,0:T(8,128)S(1)}, f32[22,128]{1,0:T(8,128)S(1)}, u32[]{:S(2)}, u32[]{:S(2)}) collective-permute-start(f32[22,128]{1,0:T(8,128)S(1)} %maximum_bitcast_fusion), channel_id=1, source_target_pairs={{0,8},{8,0},{16,24},{24,16},{32,40},{40,32},{48,56},{56,48},{64,72... | collective-permute-start | bytes 33800 | tf_op jit(solution)/shard_map/ppermute | solution.py:26
  200.2 5.3 %collective-permute-start.28 = (f32[22,128]{1,0:T(8,128)S(1)}, f32[22,128]{1,0:T(8,128)S(1)}, u32[]{:S(2)}, u32[]{:S(2)}) collective-permute-start(f32[22,128]{1,0:T(8,128)S(1)} %fusion.112), channel_id=1, source_target_pairs={{0,32},{8,40},{16,48},{24,56},{32,0},{40,8},{48,16},{56,24},{64,96... | collective-permute-start | bytes 33800 | tf_op jit(solution)/shard_map/ppermute | solution.py:22
  200.3 5.2 %collective-permute-start.27 = (f32[22,128]{1,0:T(8,128)S(1)}, f32[22,128]{1,0:T(8,128)S(1)}, u32[]{:S(2)}, u32[]{:S(2)}) collective-permute-start(f32[22,128]{1,0:T(8,128)S(1)} %fusion.112), channel_id=1, source_target_pairs={{0,48},{8,56},{16,0},{24,8},{32,16},{40,24},{48,32},{56,40},{64,11... | collective-permute-start | bytes 33800 | tf_op jit(solution)/shard_map/ppermute | solution.py:22
  203.8 4.9 %collective-permute-start.26 = (f32[22,128]{1,0:T(8,128)S(1)}, f32[22,128]{1,0:T(8,128)S(1)}, u32[]{:S(2)}, u32[]{:S(2)}) collective-permute-start(f32[22,128]{1,0:T(8,128)S(1)} %fusion.112), channel_id=1, source_target_pairs={{0,16},{8,24},{16,32},{24,40},{32,48},{40,56},{48,0},{56,8},{64,80... | collective-permute-start | bytes 33800 | tf_op jit(solution)/shard_map/ppermute | solution.py:22
  209.3 7.4 %collective-permute-start.29 = (f32[22,128]{1,0:T(8,128)}, f32[22,128]{1,0:T(8,128)S(1)}, u32[]{:S(2)}, u32[]{:S(2)}) collective-permute-start(f32[22,128]{1,0:T(8,128)} %add_add_fusion), channel_id=1, source_target_pairs={{0,68},{4,64},{8,76},{12,72},{16,84},{20,80},{24,92},{28,88},{32,1... | collective-permute-start | bytes 33800 | tf_op jit(solution)/shard_map/ppermute | solution.py:34
  212.7 25.1 %collective-permute-start.21 = (bf16[192,1024]{1,0:T(8,128)(2,1)}, bf16[192,1024]{1,0:T(8,128)(2,1)}, u32[]{:S(2)}, u32[]{:S(2)}) collective-permute-start(bf16[192,1024]{1,0:T(8,128)(2,1)} %get-tuple-element.58), channel_id=1, source_target_pairs={{0,1},{1,2},{2,3},{3,0},{4,5},{5,6},{6,7},{7,4},{8,9},{9,10},{10,1... | collective-permute-start | bytes 1179656 | tf_op jit(solution)/shard_map/ppermute | solution.py:14
  217.5 5.0 %collective-permute-start.30 = (f32[22,128]{1,0:T(8,128)S(1)}, f32[22,128]{1,0:T(8,128)S(1)}, u32[]{:S(2)}, u32[]{:S(2)}) collective-permute-start(f32[22,128]{1,0:T(8,128)S(1)} %add.380), channel_id=1, source_target_pairs={{0,4},{4,0},{1,5},{5,1},{2,6},{6,2},{3,7},{7,3},{8,12},{12,8},{9,1... | collective-permute-start | bytes 33800 | tf_op jit(solution)/shard_map/ppermute | solution.py:38
  222.5 6.8 %collective-permute-start.33 = (f32[16,128]{1,0:T(8,128)S(1)}, f32[16,128]{1,0:T(8,128)}, u32[]{:S(2)}, u32[]{:S(2)}) collective-permute-start(f32[16,128]{1,0:T(8,128)S(1)} %slice.128), channel_id=1, source_target_pairs={{0,2},{1,3},{2,0},{3,1},{4,6},{5,7},{6,4},{7,5},{8,10},{9,11},{10,... | collective-permute-start | bytes 24584 | tf_op jit(solution)/shard_map/ppermute | solution.py:14
  226.2 4.4 %collective-permute-start.32 = (f32[16,128]{1,0:T(8,128)S(1)}, f32[16,128]{1,0:T(8,128)}, u32[]{:S(2)}, u32[]{:S(2)}) collective-permute-start(f32[16,128]{1,0:T(8,128)S(1)} %slice.128), channel_id=1, source_target_pairs={{0,3},{1,0},{2,1},{3,2},{4,7},{5,4},{6,5},{7,6},{8,11},{9,8},{10,9... | collective-permute-start | bytes 24584 | tf_op jit(solution)/shard_map/ppermute | solution.py:14
  226.2 5.3 %collective-permute-start.31 = (f32[16,128]{1,0:T(8,128)S(1)}, f32[16,128]{1,0:T(8,128)}, u32[]{:S(2)}, u32[]{:S(2)}) collective-permute-start(f32[16,128]{1,0:T(8,128)S(1)} %slice.128), channel_id=1, source_target_pairs={{0,1},{1,2},{2,3},{3,0},{4,5},{5,6},{6,7},{7,4},{8,9},{9,10},{10,1... | collective-permute-start | bytes 24584 | tf_op jit(solution)/shard_map/ppermute | solution.py:14
  229.3 12.7 %collective-permute-start.20 = (bf16[192,1024]{1,0:T(8,128)(2,1)}, bf16[192,1024]{1,0:T(8,128)(2,1)}, u32[]{:S(2)}, u32[]{:S(2)}) collective-permute-start(bf16[192,1024]{1,0:T(8,128)(2,1)} %get-tuple-element.59), channel_id=1, source_target_pairs={{0,3},{1,0},{2,1},{3,2},{4,7},{5,4},{6,5},{7,6},{8,11},{9,8},{10,9... | collective-permute-start | bytes 1179656 | tf_op jit(solution)/shard_map/ppermute | solution.py:14
  230.5 11.5 %collective-permute-start.19 = (bf16[192,1024]{1,0:T(8,128)(2,1)}, bf16[192,1024]{1,0:T(8,128)(2,1)}, u32[]{:S(2)}, u32[]{:S(2)}) collective-permute-start(bf16[192,1024]{1,0:T(8,128)(2,1)} %get-tuple-element.57), channel_id=1, source_target_pairs={{0,2},{1,3},{2,0},{3,1},{4,6},{5,7},{6,4},{7,5},{8,10},{9,11},{10,... | collective-permute-start | bytes 1179656 | tf_op jit(solution)/shard_map/ppermute | solution.py:14
  231.5 32.6 %collective-permute-start.34 = (bf16[1,2,4,64,1024]{4,3,2,1,0:T(8,128)(2,1)}, bf16[1,2,4,64,1024]{4,3,2,1,0:T(8,128)(2,1)}, u32[]{:S(2)}, u32[]{:S(2)}) collective-permute-start(bf16[1,2,4,64,1024]{4,3,2,1,0:T(8,128)(2,1)} %fusion.57), channel_id=1, source_target_pairs={{0,8},{8,0},{16,24},{24,16},{32,40},{40,32},{48,56},{56,48},{64,72... | collective-permute-start | bytes 3145736 | tf_op jit(solution)/shard_map/ppermute | solution.py:26
  246.8 26.1 %collective-permute-start.22 = (bf16[192,1024]{1,0:T(8,128)(2,1)S(1)}, bf16[192,1024]{1,0:T(8,128)(2,1)S(1)}, u32[]{:S(2)}, u32[]{:S(2)}) collective-permute-start(bf16[192,1024]{1,0:T(8,128)(2,1)S(1)} %get-tuple-element.43), channel_id=1, source_target_pairs={{0,1},{1,2},{2,3},{3,0},{4,5},{5,6},{6,7},{7,4},{8,9},{9,10},{10,1... | collective-permute-start | bytes 1179656 | tf_op jit(solution)/shard_map/ppermute | solution.py:14
  260.8 16.0 %collective-permute-start.23 = (bf16[192,1024]{1,0:T(8,128)(2,1)S(1)}, bf16[192,1024]{1,0:T(8,128)(2,1)S(1)}, u32[]{:S(2)}, u32[]{:S(2)}) collective-permute-start(bf16[192,1024]{1,0:T(8,128)(2,1)S(1)} %get-tuple-element.43), channel_id=1, source_target_pairs={{0,3},{1,0},{2,1},{3,2},{4,7},{5,4},{6,5},{7,6},{8,11},{9,8},{10,9... | collective-permute-start | bytes 1179656 | tf_op jit(solution)/shard_map/ppermute | solution.py:14
  265.7 11.1 %collective-permute-start.37 = (bf16[1,2,64,1024]{3,2,1,0:T(8,128)(2,1)S(1)}, bf16[1,2,64,1024]{3,2,1,0:T(8,128)(2,1)S(1)}, u32[]{:S(2)}, u32[]{:S(2)}) collective-permute-start(bf16[1,2,64,1024]{3,2,1,0:T(8,128)(2,1)S(1)} %get-tuple-element.83), channel_id=1, source_target_pairs={{0,32},{8,40},{16,48},{24,56},{32,0},{40,8},{48,16},{56,24},{64,96... | collective-permute-start | bytes 786440 | tf_op jit(solution)/shard_map/ppermute | solution.py:22
  269.3 38.9 %collective-permute-start.43 = (bf16[3,2,64,1152]{3,2,0,1:T(8,128)(2,1)S(1)}, bf16[3,2,64,1152]{3,2,0,1:T(8,128)(2,1)S(1)}, u32[]{:S(2)}, u32[]{:S(2)}) collective-permute-start(bf16[3,2,64,1152]{3,2,0,1:T(8,128)(2,1)S(1)} %get-tuple-element.55), channel_id=1, source_target_pairs={{0,32},{8,40},{16,48},{24,56},{32,0},{40,8},{48,16},{56,24},{64,96... | collective-permute-start | bytes 2654216 | tf_op jit(solution)/shard_map/ppermute | solution.py:22
  272.9 35.3 %collective-permute-start.42 = (bf16[3,2,64,1152]{3,2,0,1:T(8,128)(2,1)S(1)}, bf16[3,2,64,1152]{3,2,0,1:T(8,128)(2,1)S(1)}, u32[]{:S(2)}, u32[]{:S(2)}) collective-permute-start(bf16[3,2,64,1152]{3,2,0,1:T(8,128)(2,1)S(1)} %get-tuple-element.56), channel_id=1, source_target_pairs={{0,16},{8,24},{16,32},{24,40},{32,48},{40,56},{48,0},{56,8},{64,80... | collective-permute-start | bytes 2654216 | tf_op jit(solution)/shard_map/ppermute | solution.py:22
  272.9 35.3 %collective-permute-start.41 = (bf16[3,2,64,1152]{3,2,0,1:T(8,128)(2,1)S(1)}, bf16[3,2,64,1152]{3,2,0,1:T(8,128)(2,1)S(1)}, u32[]{:S(2)}, u32[]{:S(2)}) collective-permute-start(bf16[3,2,64,1152]{3,2,0,1:T(8,128)(2,1)S(1)} %get-tuple-element.54), channel_id=1, source_target_pairs={{0,48},{8,56},{16,0},{24,8},{32,16},{40,24},{48,32},{56,40},{64,11... | collective-permute-start | bytes 2654216 | tf_op jit(solution)/shard_map/ppermute | solution.py:22
  276.7 29.4 %collective-permute-start.36 = (bf16[1,2,64,1024]{3,2,1,0:T(8,128)(2,1)S(1)}, bf16[1,2,64,1024]{3,2,1,0:T(8,128)(2,1)S(1)}, u32[]{:S(2)}, u32[]{:S(2)}) collective-permute-start(bf16[1,2,64,1024]{3,2,1,0:T(8,128)(2,1)S(1)} %get-tuple-element.84), channel_id=1, source_target_pairs={{0,16},{8,24},{16,32},{24,40},{32,48},{40,56},{48,0},{56,8},{64,80... | collective-permute-start | bytes 786440 | tf_op jit(solution)/shard_map/ppermute | solution.py:22
  276.7 30.8 %collective-permute-start.35 = (bf16[1,2,64,1024]{3,2,1,0:T(8,128)(2,1)S(1)}, bf16[1,2,64,1024]{3,2,1,0:T(8,128)(2,1)S(1)}, u32[]{:S(2)}, u32[]{:S(2)}) collective-permute-start(bf16[1,2,64,1024]{3,2,1,0:T(8,128)(2,1)S(1)} %get-tuple-element.82), channel_id=1, source_target_pairs={{0,48},{8,56},{16,0},{24,8},{32,16},{40,24},{48,32},{56,40},{64,11... | collective-permute-start | bytes 786440 | tf_op jit(solution)/shard_map/ppermute | solution.py:22
  306.1 9.3 %collective-permute-start.24 = (bf16[192,1024]{1,0:T(8,128)(2,1)S(1)}, bf16[192,1024]{1,0:T(8,128)(2,1)S(1)}, u32[]{:S(2)}, u32[]{:S(2)}) collective-permute-start(bf16[192,1024]{1,0:T(8,128)(2,1)S(1)} %get-tuple-element.43), channel_id=1, source_target_pairs={{0,2},{1,3},{2,0},{3,1},{4,6},{5,7},{6,4},{7,5},{8,10},{9,11},{10,... | collective-permute-start | bytes 1179656 | tf_op jit(solution)/shard_map/ppermute | solution.py:14
  307.7 7.7 %collective-permute-start.38 = (bf16[1,64,1024]{2,1,0:T(8,128)(2,1)S(1)}, bf16[1,64,1024]{2,1,0:T(8,128)(2,1)S(1)}, u32[]{:S(2)}, u32[]{:S(2)}) collective-permute-start(bf16[1,64,1024]{2,1,0:T(8,128)(2,1)S(1)} %dynamic-slice_bitcast_fusion.11), channel_id=1, source_target_pairs={{0,68},{4,64},{8,76},{12,72},{16,84},{20,80},{24,92},{28,88},{32,1... | collective-permute-start | bytes 393224 | tf_op jit(solution)/shard_map/ppermute | solution.py:34
  308.7 13.2 %collective-permute-start.44 = (bf16[3,64,1152]{2,1,0:T(8,128)(2,1)S(1)}, bf16[3,64,1152]{2,1,0:T(8,128)(2,1)S(1)}, u32[]{:S(2)}, u32[]{:S(2)}) collective-permute-start(bf16[3,64,1152]{2,1,0:T(8,128)(2,1)S(1)} %dynamic-slice_bitcast_fusion.3), channel_id=1, source_target_pairs={{0,68},{4,64},{8,76},{12,72},{16,84},{20,80},{24,92},{28,88},{32,1... | collective-permute-start | bytes 1327112 | tf_op jit(solution)/shard_map/ppermute | solution.py:34
  315.5 6.7 %collective-permute-start.39 = (bf16[1,64,1024]{2,1,0:T(8,128)(2,1)S(1)}, bf16[1,64,1024]{2,1,0:T(8,128)(2,1)S(1)}, u32[]{:S(2)}, u32[]{:S(2)}) collective-permute-start(bf16[1,64,1024]{2,1,0:T(8,128)(2,1)S(1)} %fusion.106), channel_id=1, source_target_pairs={{0,4},{4,0},{1,5},{5,1},{2,6},{6,2},{3,7},{7,3},{8,12},{12,8},{9,1... | collective-permute-start | bytes 393224 | tf_op jit(solution)/shard_map/ppermute | solution.py:38
  322.1 9.3 %collective-permute-start.45 = (bf16[3,64,1152]{2,1,0:T(8,128)(2,1)S(1)}, bf16[3,64,1152]{2,1,0:T(8,128)(2,1)S(1)}, u32[]{:S(2)}, u32[]{:S(2)}) collective-permute-start(bf16[3,64,1152]{2,1,0:T(8,128)(2,1)S(1)} %fusion.62), channel_id=1, source_target_pairs={{0,4},{4,0},{1,5},{5,1},{2,6},{6,2},{3,7},{7,3},{8,12},{12,8},{9,1... | collective-permute-start | bytes 1327112 | tf_op jit(solution)/shard_map/ppermute | solution.py:38
  (64 other events, 837.7 us)
Sparse Core Ops, SparseCore 0:
  11.1 72.4 all-gather.1
  235.1 53.7 all-reduce.1

commit v2 on v1

--- a/solution.py
+++ b/solution.py
@@ -73,6 +73,20 @@
     return [v, x_shift(v, 1), x_shift(v, -1), x_shift(v, 2)]
 
 
+def tie(v, *deps):
+    return lax.optimization_barrier((v,) + deps)[0]
+
+
+def split(v):
+    high = v.astype(BF)
+    return jnp.concatenate([high, (v - high.astype(F32)).astype(BF)], 0)
+
+
+def joined(v):
+    half = v.shape[0] // 2
+    return v[:half].astype(F32) + v[half:].astype(F32)
+
+
 def scatter_x(parts):
     got = [
         x_shift(parts[3].astype(BF), 2),
@@ -80,6 +94,27 @@
         x_shift(parts[2].astype(BF), 1),
     ]
     return parts[0] + got[0].astype(F32) + got[1].astype(F32) + got[2].astype(F32)
+
+
+def core_stage(g, core):
+    g = g.transpose(3, 1, 2, 0, 4, 5)
+    send = lax.dynamic_index_in_dim(g, 1 - core, 0, False)
+    keep = lax.dynamic_index_in_dim(g, core, 0, False)
+    return (keep.astype(F32) + core_swap(send).astype(F32)).astype(BF)
+
+
+def y_stage(h, y):
+    at = lambda d: lax.dynamic_index_in_dim(h, (y + d) % 4, 1, False)
+    opp, up, down = at(2), at(1), at(3)
+    from_down = y_shift(opp[0], 1)
+    from_up = y_shift(opp[1], -1)
+    up = jnp.concatenate([(up[0].astype(F32) + from_down.astype(F32)).astype(BF)[None], up[1:]], 0)
+    down = jnp.concatenate(
+        [down[:1], (down[1].astype(F32) + from_up.astype(F32)).astype(BF)[None]], 0
+    )
+    one = y_shift(up, 1)
+    two = y_shift(down, -1)
+    return (at(0).astype(F32) + one.astype(F32) + two.astype(F32)).astype(BF)
 
 
 def body(
@@ -160,43 +195,89 @@
     out_part = place([f.astype(BF) for f in ffns], spots)
     result = lax.psum(out_part, "tp").reshape(in_shape)
     grad_mid_in = scatter_x(mids)
-    nm_all = jnp.concatenate(nm, 0)
-    cot_all = jnp.concatenate(cots, 0)
+    nm_all = tie(jnp.concatenate(nm, 0), *mids)
+    cot_all = tie(jnp.concatenate(cots, 0), *mids)
     act_all = jnp.concatenate(acts, 0)
     gg_all = jnp.concatenate(ggs, 0)
     gu_all = jnp.concatenate(gus, 0)
     g_ffn = jnp.stack(
         [dot(nm_all, gg_all, RR), dot(nm_all, gu_all, RR), dot(cot_all, act_all, RR)], 0
     ).astype(BF)
+    h_ffn = core_stage(g_ffn.reshape(3, 2, 4, 2, 64, 1152), core)
 
     cot_own = cots[0].astype(F32)
     sv = grad_mid_in * gain2
     grad_middle = cot_own + inv2 * (sv - normed2 * jnp.mean(sv * normed2, -1, keepdims=True))
     gain2_part = jnp.sum(grad_mid_in * normed2, 0)
-    grad_branch = place(gather_x(grad_middle.astype(BF)), spots)
-
-    grad_gated = dot(grad_branch, w_out_t)
-    g_out_t = dot(grad_branch, gated, RR)
+    grad_branch = tie(grad_middle.astype(BF), h_ffn)
+    branches = gather_x(grad_branch)
+    h_ffn = tie(h_ffn, grad_branch)
+    k_ffn = y_stage(h_ffn, y)
+
+    grad_gated = place([dot(p, w_out_t) for p in branches], spots)
     grad_c = grad_gated * conv_out
     grad_conv = grad_gated * gate_c
-    taps_part = jnp.stack(
-        [
-            jnp.sum(extended[:rows] * grad_conv, 0),
-            jnp.sum(extended[1 : rows + 1] * grad_conv, 0),
-            jnp.sum(extended[2:] * grad_conv, 0),
-        ],
-        0,
-    )
     back = passed_along(grad_conv[:2], -1)
     padded = jnp.concatenate([grad_conv, back], 0)
     grad_mixed = taps[2] * padded[:rows] + taps[1] * padded[1 : rows + 1] + taps[0] * padded[2:]
     rounded = grad_mixed.astype(BF).astype(F32)
     grad_proj = jnp.concatenate([rounded * values_v, grad_c, rounded * gate_b], 1).astype(BF)
-    norm_part = dot(grad_proj, w_in, CC)
-    gain1_part = jnp.sum(norm_part * normed1, 0)
-    grad_norm_in = scatter_x([block(norm_part, s) for s in spots])
-    g_in = dot(normed_in, grad_proj, RR)
+    norm_parts = [dot(block(grad_proj, s), w_in, CC) for s in spots]
+    grad_norm_in = scatter_x(norm_parts)
+
+    grad_proj_late = tie(grad_proj, *norm_parts)
+    branch_all = tie(jnp.concatenate(branches, 0), *norm_parts)
+    grad_conv_late = tie(grad_conv, *norm_parts)
+    g_out_t = dot(branch_all, jnp.concatenate([block(gated, s) for s in spots], 0), RR)
+    g_in = dot(normed_in, grad_proj_late, RR)
     g_mix = jnp.concatenate([g_in, g_out_t], 1).astype(BF)
+    taps_part = jnp.stack(
+        [
+            jnp.sum(extended[:rows] * grad_conv_late, 0),
+            jnp.sum(extended[1 : rows + 1] * grad_conv_late, 0),
+            jnp.sum(extended[2:] * grad_conv_late, 0),
+        ],
+        0,
+    )
+    gain1_part = sum(
+        jnp.sum(p * block(normed1, s), 0) for p, s in zip(norm_parts, spots)
+    )
+    small = jnp.concatenate(
+        [gain1_part, gain2_part, taps_part.reshape(-1), jnp.zeros((256,), F32)], 0
+    ).reshape(3, 1024)
+    small = jnp.concatenate([small, jnp.zeros((5, 1024), F32)], 0)
+
+    g_mix = g_mix.reshape(2, 4, 2, 64, 1024)
+    send = lax.dynamic_index_in_dim(g_mix, 1 - core, 2, False).reshape(512, 1024)
+    keep = lax.dynamic_index_in_dim(g_mix, core, 2, False).reshape(512, 1024)
+    got = core_swap(jnp.concatenate([send, split(small)], 0))
+    h = (keep.astype(F32) + got[:512].astype(F32)).astype(BF).reshape(2, 4, 64, 1024)
+    small = small + joined(got[512:])
+    small_y = split(small)
+
+    def y_piece(d):
+        piece = lax.dynamic_index_in_dim(h, (y + d) % 4, 1, False).reshape(128, 1024)
+        return y_shift(jnp.concatenate([piece, small_y], 0), d)
+
+    k = lax.dynamic_index_in_dim(h, y, 1, False).reshape(128, 1024).astype(F32)
+    for got in (y_piece(2), y_piece(1), y_piece(3)):
+        k = k + got[:128].astype(F32)
+        small = small + joined(got[128:])
+    k = k.astype(BF).reshape(2, 64, 1024)
+    far = lax.dynamic_index_in_dim(k, 1 - zh, 0, False)
+    got = z_cross(jnp.concatenate([far, split(small)], 0))
+    half = (lax.dynamic_index_in_dim(k, zh, 0, False).astype(F32) + got[:64].astype(F32)).astype(BF)
+    small = small + joined(got[64:])
+    got = ctx_swap(jnp.concatenate([half, split(small)], 0))
+    r_mix = half.astype(F32) + got[:64].astype(F32)
+    small = small + joined(got[64:])
+    gains = small[:2].reshape(16, 128)
+    gains = gains + x_shift(gains, 1) + x_shift(gains, -1) + x_shift(gains, 2)
+
+    own = lax.dynamic_index_in_dim(k_ffn, zh, 0, False).astype(F32)
+    far = lax.dynamic_index_in_dim(k_ffn, 1 - zh, 0, False)
+    half = (own + z_cross(far).astype(F32)).astype(BF)
+    r_ffn = half.astype(F32) + ctx_swap(half).astype(F32)
 
     inv1_own = inv_rms_of(own_tok)
     normed1_own = own_tok * inv1_own
@@ -206,40 +287,12 @@
     )
     input_grad = place(gather_x(grad_rows.astype(BF)), spots).reshape(in_shape)
 
-    def reduce_grads(g):
-        n, _, m = g.shape
-        g = g.reshape(n, 2, 4, 2, 64, m)
-        send = lax.dynamic_index_in_dim(g, 1 - core, 3, False)
-        keep = lax.dynamic_index_in_dim(g, core, 3, False)
-        h = (keep.astype(F32) + core_swap(send).astype(F32)).astype(BF)
-        part = [lax.dynamic_index_in_dim(h, s, 2, False) for s in (y, (y + 3) % 4, (y + 1) % 4, (y + 2) % 4)]
-        k = (
-            part[0].astype(F32)
-            + y_shift(part[1], -1).astype(F32)
-            + y_shift(part[2], 1).astype(F32)
-            + y_shift(part[3], 2).astype(F32)
-        ).astype(BF)
-        own = lax.dynamic_index_in_dim(k, zh, 1, False).astype(F32)
-        far = lax.dynamic_index_in_dim(k, 1 - zh, 1, False)
-        half = (own + z_cross(far).astype(F32)).astype(BF)
-        return half.astype(F32) + ctx_swap(half).astype(F32)
-
-    r_ffn = reduce_grads(g_ffn)
-    r_mix = reduce_grads(g_mix[None])[0]
-
-    small = jnp.concatenate([gain1_part, gain2_part, taps_part.reshape(-1)], 0).reshape(22, 128)
-    small = small + core_swap(small)
-    small = small + y_shift(small, 1) + y_shift(small, -1) + y_shift(small, 2)
-    small = small + z_cross(small)
-    small = small + ctx_swap(small)
-    gains = small[:16]
-    gains = gains + x_shift(gains, 1) + x_shift(gains, -1) + x_shift(gains, 2)
     return (
         result,
         input_grad,
         gains[:8].reshape(-1),
         r_mix[:, :768].reshape(64, 3, 256),
-        small[16:].reshape(3, 256),
+        small[2, :768].reshape(3, 256),
         r_mix[:, 768:].T,
         gains[8:].reshape(-1),
         r_ffn[:2],

time: 346 us -> 344 us (level)
  starting transfers between devices: 93.1 us -> 71 us
  waiting for transfers between devices: 121 us -> 140 us
    ppermute x21, waiting for transfers between devices: 50.3 us -> 94.5 us  [x_shift(): return lax.ppermute(v, 'tp', [(i, (i + d) % NX) for i in range(NX)])]
    ppermute x12 -> x10, waiting for transfers between devices: 46.8 us -> 23.3 us  [y_shift(): return lax.ppermute(v, 'fsdp', route)]
    ppermute x21, starting transfers between devices: 59.3 us -> 42.9 us  [x_shift(): return lax.ppermute(v, 'tp', [(i, (i + d) % NX) for i in range(NX)])]
    concatenate x0 -> x12, other arithmetic: none -> 6.51 us  [the longest x1 1.38 us: body(): cot_all = tie(jnp.concatenate(cots, 0), *mids)]
    ppermute x12 -> x10, starting transfers between devices: 19 us -> 13.8 us  [y_shift(): return lax.ppermute(v, 'fsdp', route)]
    convert_element_type x6 -> x11, other arithmetic: 5.6 us -> 9.39 us  [the longest x1 4.3 us: core_stage(): return (keep.astype(F32) + core_swap(send).astype(F32)).astype(BF)]
    ppermute x3 -> x2, waiting for transfers between devices: 7.81 us -> 4.53 us  [ctx_swap(): return lax.ppermute(v, 'ctx', [(0, 1), (1, 0)])]
    ppermute x4 -> x3, waiting for transfers between devices: 9.04 us -> 11.9 us  [z_cross(): return lax.ppermute(v, ('fsdp', 'ctx'), route)]
  transfers between devices with their start and end apart: 48 -> 43, of which waited for: 20 -> 28; matrix products, arithmetic and copies ran while one was open for 30% -> 24% of each run, Pallas kernels for 0% -> 0%
where the time goes in v2:
time: 344 us; the launch traced here: 341 us
  waiting for transfers between devices  140 us (41%)
  starting transfers between devices  71 us (21%)
  matrix products  52.9 us (15%)
  other arithmetic  31.1 us (9%)
  local copies, waits for them, and re-layouts  29.8 us (9%)
  between operations  15.7 us (5%)
    ppermute x21, waiting for transfers between devices, x_shift(): return lax.ppermute(v, 'tp', [(i, (i + d) % NX) for i in range(NX)])  94.5 us
    dot_general x39, matrix products, dot(): return lax.dot_general(a, b, dims, preferred_element_type=F32)  52.9 us
    ppermute x21, starting transfers between devices, x_shift(): return lax.ppermute(v, 'tp', [(i, (i + d) % NX) for i in range(NX)])  42.9 us
    ppermute x10, waiting for transfers between devices, y_shift(): return lax.ppermute(v, 'fsdp', route)  23.3 us
    ppermute x10, starting transfers between devices, y_shift(): return lax.ppermute(v, 'fsdp', route)  13.8 us
    ppermute x3, waiting for transfers between devices, z_cross(): return lax.ppermute(v, ('fsdp', 'ctx'), route)  11.9 us
    unnamed x104, local copies, waits for them, and re-layouts  10.6 us
    ppermute x3, starting transfers between devices, z_cross(): return lax.ppermute(v, ('fsdp', 'ctx'), route)  9.72 us
  transfers between devices with their start and end apart: 43, of which 28 were waited for; matrix products, arithmetic and copies ran while one was open for 24% of the time, Pallas kernels for 0%

profile of v2, /device:TPU:0, one launch (start us, length us, event | category | flops | bytes accessed | tf_op | source)
XLA Modules:
  0.0 340.8 jit_solution(16188787318464360101)
XLA Ops:
  11.0 4.2 %collective-permute-start = (bf16[64,1024]{1,0:T(8,128)(2,1)S(1)}, bf16[64,1024]{1,0:T(8,128)(2,1)S(1)}, u32[]{:S(2)}, u32[]{:S(2)}) collective-permute-start(bf16[64,1024]{1,0:T(8,128)(2,1)S(1)} %pad_maximum_fusion.18), channel_id=1, source_target_pairs={{0,68},{4,64},{8,76},{12,72},{16,84},{20,80},{24,92},{28,88},{32,1... | collective-permute-start | bytes 393224 | tf_op jit(solution)/shard_map/ppermute | solution.py:34
  16.0 2.7 collective-permute-done
  24.1 5.3 %collective-permute-done.1 = bf16[2,64,1024]{2,1,0:T(8,128)(2,1)S(1)} collective-permute-done((bf16[2,64,1024]{2,1,0:T(8,128)(2,1)S(1)}, bf16[2,64,1024]{2,1,0:T(8,128)(2,1)S(1)}, u32[]{:S(2)}, u32[]{:S(2)}) %collective-permute-start.1) | collective-permute-done | bytes 262176 | tf_op jit(solution)/shard_map/ppermute | solution.py:22
  29.5 5.0 %collective-permute-done.2 = bf16[2,64,1024]{2,1,0:T(8,128)(2,1)S(1)} collective-permute-done((bf16[2,64,1024]{2,1,0:T(8,128)(2,1)S(1)}, bf16[2,64,1024]{2,1,0:T(8,128)(2,1)S(1)}, u32[]{:S(2)}, u32[]{:S(2)}) %collective-permute-start.2) | collective-permute-done | bytes 262176 | tf_op jit(solution)/shard_map/ppermute | solution.py:22
  34.5 6.9 %collective-permute-done.3 = bf16[2,64,1024]{2,1,0:T(8,128)(2,1)S(1)} collective-permute-done((bf16[2,64,1024]{2,1,0:T(8,128)(2,1)S(1)}, bf16[2,64,1024]{2,1,0:T(8,128)(2,1)S(1)}, u32[]{:S(2)}, u32[]{:S(2)}) %collective-permute-start.3) | collective-permute-done | bytes 262176 | tf_op jit(solution)/shard_map/ppermute | solution.py:22
  51.3 2.3 multiply_convert_fusion.15
  62.1 7.4 %collective-permute-done.8 = bf16[192,1024]{1,0:T(8,128)(2,1)S(1)} collective-permute-done((bf16[192,1024]{1,0:T(8,128)(2,1)}, bf16[192,1024]{1,0:T(8,128)(2,1)S(1)}, u32[]{:S(2)}, u32[]{:S(2)}) %collective-permute-start.8) | collective-permute-done | bytes 393248 | tf_op jit(solution)/shard_map/ppermute | solution.py:14
  69.5 7.4 %collective-permute-done.7 = bf16[192,1024]{1,0:T(8,128)(2,1)} collective-permute-done((bf16[192,1024]{1,0:T(8,128)(2,1)}, bf16[192,1024]{1,0:T(8,128)(2,1)}, u32[]{:S(2)}, u32[]{:S(2)}) %collective-permute-start.7) | collective-permute-done | bytes 393248 | tf_op jit(solution)/shard_map/ppermute | solution.py:14
  86.7 14.3 %collective-permute-done.9 = bf16[192,1024]{1,0:T(8,128)(2,1)S(1)} collective-permute-done((bf16[192,1024]{1,0:T(8,128)(2,1)S(1)}, bf16[192,1024]{1,0:T(8,128)(2,1)S(1)}, u32[]{:S(2)}, u32[]{:S(2)}) %collective-permute-start.9) | collective-permute-done | bytes 393248 | tf_op jit(solution)/shard_map/ppermute | solution.py:14
  103.9 2.6 fusion.89
  106.6 2.7 fusion.86
  112.2 12.7 %collective-permute-start.14 = (bf16[192,1024]{1,0:T(8,128)(2,1)S(1)}, bf16[192,1024]{1,0:T(8,128)(2,1)S(1)}, u32[]{:S(2)}, u32[]{:S(2)}) collective-permute-start(bf16[192,1024]{1,0:T(8,128)(2,1)S(1)} %convolution_add_fusion), channel_id=1, source_target_pairs={{0,1},{1,2},{2,3},{3,0},{4,5},{5,6},{6,7},{7,4},{8,9},{9,10},{10,1... | collective-permute-start | bytes 1179656 | tf_op jit(solution)/shard_map/ppermute | solution.py:14
  129.3 3.3 collective-permute-start.13
  141.7 4.6 %collective-permute-done.13 = bf16[192,1024]{1,0:T(8,128)(2,1)S(1)} collective-permute-done((bf16[192,1024]{1,0:T(8,128)(2,1)S(1)}, bf16[192,1024]{1,0:T(8,128)(2,1)S(1)}, u32[]{:S(2)}, u32[]{:S(2)}) %collective-permute-start.13) | collective-permute-done | bytes 393248 | tf_op jit(solution)/shard_map/ppermute | solution.py:14
  146.3 2.1 multiply_reduce_fusion.3
  148.4 2.3 convolution_convert_fusion.1
  150.8 2.3 convolution_convert_fusion.2
  153.1 2.3 convolution_convert_fusion
  156.5 2.4 constant_dynamic-slice_fusion.9
  161.4 4.0 %fusion.71 = (bf16[1024,768]{0,1:T(8,128)(2,1)}, f32[768,1024]{1,0:T(8,128)}) fusion(f32[1024]{0:T(1024)S(1)} %convert_element_type.354, f32[768]{0:T(1024)S(1)} %add_rsqrt_fusion, bf16[1,768,1024]{2,1,0:T(8,128)(2,1)} %param.9), kind=kLoop, calls=%fused_computation.162 | loop fusion | flops 3145728 | bytes 6298624 | tf_op jit(solution)/shard_map/dot_general | solution.py:47
  165.4 2.6 copy.44
  171.2 3.4 %fusion.28 = bf16[1,768,1024]{2,1,0:T(8,128)(2,1)} fusion(bf16[1,768,1024]{2,1,0:T(8,128)(2,1)} %broadcast.78.clone, s32[]{:T(128)S(6)} %select_n.147, f32[192,1024]{1,0:T(8,128)S(1)} %copy-done.4, bf16[192,1152]{1,0:T(8,128)(2,1)S(1)} %copy-done.44, bf16[3,1024,1152]{2,1,0:T(8,128)(2,1)} %all-gather.2.cloned.1.call-done), kind=kOutput, calls=%fused_computation.59 | convolution fusion | flops 453378048 | bytes 3981316 | tf_op jit(solution)/shard_map/dot_general | solution.py:47
  174.6 3.4 %fusion.30 = bf16[1,768,1024]{2,1,0:T(8,128)(2,1)} fusion(bf16[1,768,1024]{2,1,0:T(8,128)(2,1)} %fusion.28, s32[]{:T(128)S(6)} %select_n.166, bf16[192,1152]{1,0:T(8,128)(2,1)S(1)} %copy-done.48, bf16[3,1024,1152]{2,1,0:T(8,128)(2,1)} %all-gather.2.cloned.1.call-done), kind=kOutput, calls=%fused_computation.61 | convolution fusion | flops 453181440 | bytes 3194884 | tf_op jit(solution)/shard_map/dot_general | solution.py:47
  178.0 3.4 fusion.32
  181.4 3.3 fusion.34
  186.5 4.3 %fusion = bf16[2,4,3,64,1152]{4,3,2,0,1:T(8,128)(2,1)S(1)} fusion(bf16[2,4,3,64,1152]{4,3,2,0,1:T(8,128)(2,1)} %collective-permute-done.15, bf16[3,2,4,1,64,1152]{5,4,3,2,1,0:T(8,128)(2,1)} %get-tuple-element.67), kind=kLoop, calls=%fused_computation.2 | loop fusion | flops 7077888 | bytes 10616832 | tf_op jit(solution)/shard_map/convert_element_type | solution.py:103
  190.8 2.7 collective-permute-start.16
  197.2 2.3 collective-permute-start.37
  199.9 10.8 %collective-permute-done.16 = bf16[192,1024]{1,0:T(8,128)(2,1)S(1)} collective-permute-done((bf16[192,1024]{1,0:T(8,128)(2,1)S(1)}, bf16[192,1024]{1,0:T(8,128)(2,1)S(1)}, u32[]{:S(2)}, u32[]{:S(2)}) %collective-permute-start.16) | collective-permute-done | bytes 393248 | tf_op jit(solution)/shard_map/ppermute | solution.py:14
  211.0 2.5 collective-permute-done.17
  213.8 12.8 %collective-permute-done.18 = bf16[192,1024]{1,0:T(8,128)(2,1)S(1)} collective-permute-done((bf16[192,1024]{1,0:T(8,128)(2,1)S(1)}, bf16[192,1024]{1,0:T(8,128)(2,1)S(1)}, u32[]{:S(2)}, u32[]{:S(2)}) %collective-permute-start.18) | collective-permute-done | bytes 393248 | tf_op jit(solution)/shard_map/ppermute | solution.py:14
  229.7 2.9 collective-permute-done.19
  235.6 2.2 collective-permute-start.21
  243.2 11.8 %collective-permute-done.22 = bf16[192,1024]{1,0:T(8,128)(2,1)S(1)} collective-permute-done((bf16[192,1024]{1,0:T(8,128)(2,1)S(1)}, bf16[192,1024]{1,0:T(8,128)(2,1)S(1)}, u32[]{:S(2)}, u32[]{:S(2)}) %collective-permute-start.22) | collective-permute-done | bytes 393248 | tf_op jit(solution)/shard_map/ppermute | solution.py:14
  255.0 3.7 %collective-permute-done.21 = bf16[192,1024]{1,0:T(8,128)(2,1)S(1)} collective-permute-done((bf16[192,1024]{1,0:T(8,128)(2,1)S(1)}, bf16[192,1024]{1,0:T(8,128)(2,1)S(1)}, u32[]{:S(2)}, u32[]{:S(2)}) %collective-permute-start.21) | collective-permute-done | bytes 393248 | tf_op jit(solution)/shard_map/ppermute | solution.py:14
  258.7 6.8 %collective-permute-done.20 = bf16[192,1024]{1,0:T(8,128)(2,1)S(1)} collective-permute-done((bf16[192,1024]{1,0:T(8,128)(2,1)S(1)}, bf16[192,1024]{1,0:T(8,128)(2,1)S(1)}, u32[]{:S(2)}, u32[]{:S(2)}) %collective-permute-start.20) | collective-permute-done | bytes 393248 | tf_op jit(solution)/shard_map/ppermute | solution.py:14
  272.7 2.9 convolution_convert_fusion.3
  276.7 3.4 collective-permute-done.23
  281.1 3.7 %collective-permute-done.24 = bf16[192,1024]{1,0:T(8,128)(2,1)} collective-permute-done((bf16[192,1024]{1,0:T(8,128)(2,1)S(1)}, bf16[192,1024]{1,0:T(8,128)(2,1)}, u32[]{:S(2)}, u32[]{:S(2)}) %collective-permute-start.24) | collective-permute-done | bytes 393248 | tf_op jit(solution)/shard_map/ppermute | solution.py:14
  286.6 2.6 fusion.25
  289.3 5.1 %collective-permute-start.39 = (bf16[3,64,1152]{2,1,0:T(8,128)(2,1)S(1)}, bf16[3,64,1152]{2,1,0:T(8,128)(2,1)S(1)}, u32[]{:S(2)}, u32[]{:S(2)}) collective-permute-start(bf16[3,64,1152]{2,1,0:T(8,128)(2,1)S(1)} %dynamic-slice_bitcast_fusion.6), channel_id=1, source_target_pairs={{0,68},{4,64},{8,76},{12,72},{16,84},{20,80},{24,92},{28,88},{32,1... | collective-permute-start | bytes 1327112 | tf_op jit(solution)/shard_map/ppermute | solution.py:34
  298.2 3.9 %collective-permute-done.39 = bf16[3,64,1152]{2,1,0:T(8,128)(2,1)S(1)} collective-permute-done((bf16[3,64,1152]{2,1,0:T(8,128)(2,1)S(1)}, bf16[3,64,1152]{2,1,0:T(8,128)(2,1)S(1)}, u32[]{:S(2)}, u32[]{:S(2)}) %collective-permute-start.39) | collective-permute-done | bytes 442400 | tf_op jit(solution)/shard_map/ppermute | solution.py:34
  304.3 5.3 %collective-permute-done.28 = bf16[144,1024]{1,0:T(8,128)(2,1)S(1)} collective-permute-done((bf16[144,1024]{1,0:T(8,128)(2,1)S(1)}, bf16[144,1024]{1,0:T(8,128)(2,1)S(1)}, u32[]{:S(2)}, u32[]{:S(2)}) %collective-permute-start.28) | collective-permute-done | bytes 294944 | tf_op jit(solution)/shard_map/ppermute | solution.py:22
  311.2 5.3 %collective-permute-done.30 = bf16[80,1024]{1,0:T(8,128)(2,1)S(1)} collective-permute-done((bf16[80,1024]{1,0:T(8,128)(2,1)S(1)}, bf16[80,1024]{1,0:T(8,128)(2,1)S(1)}, u32[]{:S(2)}, u32[]{:S(2)}) %collective-permute-start.30) | collective-permute-done | bytes 163872 | tf_op jit(solution)/shard_map/ppermute | solution.py:34
  318.3 3.7 %collective-permute-done.31 = bf16[80,1024]{1,0:T(8,128)(2,1)S(1)} collective-permute-done((bf16[80,1024]{1,0:T(8,128)(2,1)S(1)}, bf16[80,1024]{1,0:T(8,128)(2,1)S(1)}, u32[]{:S(2)}, u32[]{:S(2)}) %collective-permute-start.31) | collective-permute-done | bytes 163872 | tf_op jit(solution)/shard_map/ppermute | solution.py:38
  322.4 3.2 collective-permute-start.33
  327.7 2.9 collective-permute-done.32
  331.1 2.7 copy.83
  (280 shorter events, 104.7 us)
Async XLA Ops:
  7.2 96.8 %all-gather.2.cloned.1.call-start = ((), (), s32[]{:S(2)}) async-start(), calls=%async_computation | async-start | bytes 7520256 | tf_op jit(solution)/shard_map/all_gather | solution.py:145
  9.1 32.5 %copy-start.40 = (bf16[1024]{0:T(1024)(128)(2,1)S(1)}, bf16[1024]{0:T(1024)(128)(2,1)}, u32[]{:S(2)}) copy-start(bf16[1024]{0:T(1024)(128)(2,1)} %param.10) | copy-start | bytes 6148
  9.1 32.5 %copy-start.6 = (bf16[1,768,1024]{2,1,0:T(8,128)(2,1)S(1)}, bf16[1,768,1024]{2,1,0:T(8,128)(2,1)}, u32[]{:S(2)}) copy-start(bf16[1,768,1024]{2,1,0:T(8,128)(2,1)} %param.9) | copy-start | bytes 4718596
  9.1 322.0 %all-reduce.3.cloned.1.call-start = ((), (), s32[]{:S(2)}) async-start(), calls=%async_computation.1 | async-start | bytes 3145728 | tf_op jit(solution)/shard_map/psum | solution.py:196
  11.0 7.7 %collective-permute-start = (bf16[64,1024]{1,0:T(8,128)(2,1)S(1)}, bf16[64,1024]{1,0:T(8,128)(2,1)S(1)}, u32[]{:S(2)}, u32[]{:S(2)}) collective-permute-start(bf16[64,1024]{1,0:T(8,128)(2,1)S(1)} %pad_maximum_fusion.18), channel_id=1, source_target_pairs={{0,68},{4,64},{8,76},{12,72},{16,84},{20,80},{24,92},{28,88},{32,1... | collective-permute-start | bytes 393224 | tf_op jit(solution)/shard_map/ppermute | solution.py:34
  18.7 10.8 %collective-permute-start.1 = (bf16[2,64,1024]{2,1,0:T(8,128)(2,1)S(1)}, bf16[2,64,1024]{2,1,0:T(8,128)(2,1)S(1)}, u32[]{:S(2)}, u32[]{:S(2)}) collective-permute-start(bf16[2,64,1024]{2,1,0:T(8,128)(2,1)S(1)} %bitcast_dynamic-update-slice_fusion.10), channel_id=1, source_target_pairs={{0,16},{8,24},{16,32},{24,40},{32,48},{40,56},{48,0},{56,8},{64,80... | collective-permute-start | bytes 786440 | tf_op jit(solution)/shard_map/ppermute | solution.py:22
  20.3 14.1 %collective-permute-start.2 = (bf16[2,64,1024]{2,1,0:T(8,128)(2,1)S(1)}, bf16[2,64,1024]{2,1,0:T(8,128)(2,1)S(1)}, u32[]{:S(2)}, u32[]{:S(2)}) collective-permute-start(bf16[2,64,1024]{2,1,0:T(8,128)(2,1)S(1)} %bitcast_dynamic-update-slice_fusion.10), channel_id=1, source_target_pairs={{0,48},{8,56},{16,0},{24,8},{32,16},{40,24},{48,32},{56,40},{64,11... | collective-permute-start | bytes 786440 | tf_op jit(solution)/shard_map/ppermute | solution.py:22
  22.0 19.4 %collective-permute-start.3 = (bf16[2,64,1024]{2,1,0:T(8,128)(2,1)S(1)}, bf16[2,64,1024]{2,1,0:T(8,128)(2,1)S(1)}, u32[]{:S(2)}, u32[]{:S(2)}) collective-permute-start(bf16[2,64,1024]{2,1,0:T(8,128)(2,1)S(1)} %bitcast_dynamic-update-slice_fusion.10), channel_id=1, source_target_pairs={{0,32},{8,40},{16,48},{24,56},{32,0},{40,8},{48,16},{56,24},{64,96... | collective-permute-start | bytes 786440 | tf_op jit(solution)/shard_map/ppermute | solution.py:22
  41.4 2.9 collective-permute-start.4
  48.6 2.6 collective-permute-start.5
  57.0 12.5 %collective-permute-start.8 = (bf16[192,1024]{1,0:T(8,128)(2,1)}, bf16[192,1024]{1,0:T(8,128)(2,1)S(1)}, u32[]{:S(2)}, u32[]{:S(2)}) collective-permute-start(bf16[192,1024]{1,0:T(8,128)(2,1)} %get-tuple-element.76), channel_id=1, source_target_pairs={{0,1},{1,2},{2,3},{3,0},{4,5},{5,6},{6,7},{7,4},{8,9},{9,10},{10,1... | collective-permute-start | bytes 1179656 | tf_op jit(solution)/shard_map/ppermute | solution.py:14
  58.5 18.3 %collective-permute-start.7 = (bf16[192,1024]{1,0:T(8,128)(2,1)}, bf16[192,1024]{1,0:T(8,128)(2,1)}, u32[]{:S(2)}, u32[]{:S(2)}) collective-permute-start(bf16[192,1024]{1,0:T(8,128)(2,1)} %get-tuple-element.77), channel_id=1, source_target_pairs={{0,3},{1,0},{2,1},{3,2},{4,7},{5,4},{6,5},{7,6},{8,11},{9,8},{10,9... | collective-permute-start | bytes 1179656 | tf_op jit(solution)/shard_map/ppermute | solution.py:14
  60.3 18.3 %collective-permute-start.6 = (bf16[192,1024]{1,0:T(8,128)(2,1)}, bf16[192,1024]{1,0:T(8,128)(2,1)}, u32[]{:S(2)}, u32[]{:S(2)}) collective-permute-start(bf16[192,1024]{1,0:T(8,128)(2,1)} %get-tuple-element.75), channel_id=1, source_target_pairs={{0,2},{1,3},{2,0},{3,1},{4,6},{5,7},{6,4},{7,5},{8,10},{9,11},{10,... | collective-permute-start | bytes 1179656 | tf_op jit(solution)/shard_map/ppermute | solution.py:14
  81.5 19.5 %collective-permute-start.9 = (bf16[192,1024]{1,0:T(8,128)(2,1)S(1)}, bf16[192,1024]{1,0:T(8,128)(2,1)S(1)}, u32[]{:S(2)}, u32[]{:S(2)}) collective-permute-start(bf16[192,1024]{1,0:T(8,128)(2,1)S(1)} %multiply_convert_fusion.14), channel_id=1, source_target_pairs={{0,1},{1,2},{2,3},{3,0},{4,5},{5,6},{6,7},{7,4},{8,9},{9,10},{10,1... | collective-permute-start | bytes 1179656 | tf_op jit(solution)/shard_map/ppermute | solution.py:14
  82.9 18.1 %collective-permute-start.10 = (bf16[192,1024]{1,0:T(8,128)(2,1)S(1)}, bf16[192,1024]{1,0:T(8,128)(2,1)S(1)}, u32[]{:S(2)}, u32[]{:S(2)}) collective-permute-start(bf16[192,1024]{1,0:T(8,128)(2,1)S(1)} %multiply_convert_fusion.14), channel_id=1, source_target_pairs={{0,3},{1,0},{2,1},{3,2},{4,7},{5,4},{6,5},{7,6},{8,11},{9,8},{10,9... | collective-permute-start | bytes 1179656 | tf_op jit(solution)/shard_map/ppermute | solution.py:14
  84.8 16.2 %collective-permute-start.11 = (bf16[192,1024]{1,0:T(8,128)(2,1)S(1)}, bf16[192,1024]{1,0:T(8,128)(2,1)S(1)}, u32[]{:S(2)}, u32[]{:S(2)}) collective-permute-start(bf16[192,1024]{1,0:T(8,128)(2,1)S(1)} %multiply_convert_fusion.14), channel_id=1, source_target_pairs={{0,2},{1,3},{2,0},{3,1},{4,6},{5,7},{6,4},{7,5},{8,10},{9,11},{10,... | collective-permute-start | bytes 1179656 | tf_op jit(solution)/shard_map/ppermute | solution.py:14
  110.3 42.8 %copy-start.45 = (bf16[192,1152]{1,0:T(8,128)(2,1)}, bf16[192,1152]{1,0:T(8,128)(2,1)S(1)}, u32[]{:S(2)}) copy-start(bf16[192,1152]{1,0:T(8,128)(2,1)S(1)} %get-tuple-element.91) | copy-start | bytes 1327108
  112.2 29.4 %collective-permute-start.14 = (bf16[192,1024]{1,0:T(8,128)(2,1)S(1)}, bf16[192,1024]{1,0:T(8,128)(2,1)S(1)}, u32[]{:S(2)}, u32[]{:S(2)}) collective-permute-start(bf16[192,1024]{1,0:T(8,128)(2,1)S(1)} %convolution_add_fusion), channel_id=1, source_target_pairs={{0,1},{1,2},{2,3},{3,0},{4,5},{5,6},{6,7},{7,4},{8,9},{9,10},{10,1... | collective-permute-start | bytes 1179656 | tf_op jit(solution)/shard_map/ppermute | solution.py:14
  129.3 17.0 %collective-permute-start.13 = (bf16[192,1024]{1,0:T(8,128)(2,1)S(1)}, bf16[192,1024]{1,0:T(8,128)(2,1)S(1)}, u32[]{:S(2)}, u32[]{:S(2)}) collective-permute-start(bf16[192,1024]{1,0:T(8,128)(2,1)S(1)} %convolution_add_fusion.1), channel_id=1, source_target_pairs={{0,3},{1,0},{2,1},{3,2},{4,7},{5,4},{6,5},{7,6},{8,11},{9,8},{10,9... | collective-permute-start | bytes 1179656 | tf_op jit(solution)/shard_map/ppermute | solution.py:14
  136.9 9.4 %collective-permute-start.12 = (bf16[192,1024]{1,0:T(8,128)(2,1)S(1)}, bf16[192,1024]{1,0:T(8,128)(2,1)S(1)}, u32[]{:S(2)}, u32[]{:S(2)}) collective-permute-start(bf16[192,1024]{1,0:T(8,128)(2,1)S(1)} %convolution_add_fusion.2), channel_id=1, source_target_pairs={{0,2},{1,3},{2,0},{3,1},{4,6},{5,7},{6,4},{7,5},{8,10},{9,11},{10,... | collective-permute-start | bytes 1179656 | tf_op jit(solution)/shard_map/ppermute | solution.py:14
  160.9 25.5 %collective-permute-start.15 = (bf16[2,4,3,64,1152]{4,3,2,0,1:T(8,128)(2,1)}, bf16[2,4,3,64,1152]{4,3,2,0,1:T(8,128)(2,1)}, u32[]{:S(2)}, u32[]{:S(2)}) collective-permute-start(bf16[2,4,3,64,1152]{4,3,2,0,1:T(8,128)(2,1)} %bitcast.244), channel_id=1, source_target_pairs={{0,8},{8,0},{16,24},{24,16},{32,40},{40,32},{48,56},{56,48},{64,72... | collective-permute-start | bytes 10616840 | tf_op jit(solution)/shard_map/ppermute | solution.py:26
  190.8 47.9 %copy-start = (bf16[2,4,3,64,1152]{4,3,2,0,1:T(8,128)(2,1)}, bf16[2,4,3,64,1152]{4,3,2,0,1:T(8,128)(2,1)S(1)}, u32[]{:S(2)}) copy-start(bf16[2,4,3,64,1152]{4,3,2,0,1:T(8,128)(2,1)S(1)} %fusion) | copy-start | bytes 10616836
  190.8 19.9 %collective-permute-start.16 = (bf16[192,1024]{1,0:T(8,128)(2,1)S(1)}, bf16[192,1024]{1,0:T(8,128)(2,1)S(1)}, u32[]{:S(2)}, u32[]{:S(2)}) collective-permute-start(bf16[192,1024]{1,0:T(8,128)(2,1)S(1)} %fusion.122), channel_id=1, source_target_pairs={{0,1},{1,2},{2,3},{3,0},{4,5},{5,6},{6,7},{7,4},{8,9},{9,10},{10,1... | collective-permute-start | bytes 1179656 | tf_op jit(solution)/shard_map/ppermute | solution.py:14
  193.5 20.0 %collective-permute-start.17 = (bf16[192,1024]{1,0:T(8,128)(2,1)S(1)}, bf16[192,1024]{1,0:T(8,128)(2,1)S(1)}, u32[]{:S(2)}, u32[]{:S(2)}) collective-permute-start(bf16[192,1024]{1,0:T(8,128)(2,1)S(1)} %fusion.122), channel_id=1, source_target_pairs={{0,3},{1,0},{2,1},{3,2},{4,7},{5,4},{6,5},{7,6},{8,11},{9,8},{10,9... | collective-permute-start | bytes 1179656 | tf_op jit(solution)/shard_map/ppermute | solution.py:14
  194.7 31.9 %collective-permute-start.18 = (bf16[192,1024]{1,0:T(8,128)(2,1)S(1)}, bf16[192,1024]{1,0:T(8,128)(2,1)S(1)}, u32[]{:S(2)}, u32[]{:S(2)}) collective-permute-start(bf16[192,1024]{1,0:T(8,128)(2,1)S(1)} %fusion.122), channel_id=1, source_target_pairs={{0,2},{1,3},{2,0},{3,1},{4,6},{5,7},{6,4},{7,5},{8,10},{9,11},{10,... | collective-permute-start | bytes 1179656 | tf_op jit(solution)/shard_map/ppermute | solution.py:14
  196.1 42.6 %collective-permute-start.35 = (bf16[3,64,1152]{2,1,0:T(8,128)(2,1)S(1)}, bf16[3,64,1152]{2,1,0:T(8,128)(2,1)S(1)}, u32[]{:S(2)}, u32[]{:S(2)}) collective-permute-start(bf16[3,64,1152]{2,1,0:T(8,128)(2,1)S(1)} %get-tuple-element.71), channel_id=1, source_target_pairs={{0,16},{8,24},{16,32},{24,40},{32,48},{40,56},{48,0},{56,8},{64,80... | collective-permute-start | bytes 1327112 | tf_op jit(solution)/shard_map/ppermute | solution.py:22
  197.2 41.6 %collective-permute-start.37 = (bf16[3,64,1152]{2,1,0:T(8,128)(2,1)S(1)}, bf16[3,64,1152]{2,1,0:T(8,128)(2,1)S(1)}, u32[]{:S(2)}, u32[]{:S(2)}) collective-permute-start(bf16[3,64,1152]{2,1,0:T(8,128)(2,1)S(1)} %get-tuple-element.72), channel_id=1, source_target_pairs={{0,48},{8,56},{16,0},{24,8},{32,16},{40,24},{48,32},{56,40},{64,11... | collective-permute-start | bytes 1327112 | tf_op jit(solution)/shard_map/ppermute | solution.py:22
  227.1 5.5 %collective-permute-start.19 = (f32[2,256]{1,0:T(2,128)S(1)}, f32[2,256]{1,0:T(2,128)S(1)}, u32[]{:S(2)}, u32[]{:S(2)}) collective-permute-start(f32[2,256]{1,0:T(2,128)S(1)} %slice.251), channel_id=1, source_target_pairs={{4,0},{5,1},{6,2},{7,3},{12,8},{13,9},{14,10},{15,11},{20,16},{21,... | collective-permute-start | bytes 6152 | tf_op jit(solution)/shard_map/ppermute | solution.py:43
  233.1 32.5 %copy-start.12 = (bf16[768,768]{1,0:T(8,128)(2,1)}, bf16[768,768]{1,0:T(8,128)(2,1)S(1)}, u32[]{:S(2)}) copy-start(bf16[768,768]{1,0:T(8,128)(2,1)S(1)} %pad_maximum_fusion.4) | copy-start | bytes 3538948
  233.8 21.3 %collective-permute-start.22 = (bf16[192,1024]{1,0:T(8,128)(2,1)S(1)}, bf16[192,1024]{1,0:T(8,128)(2,1)S(1)}, u32[]{:S(2)}, u32[]{:S(2)}) collective-permute-start(bf16[192,1024]{1,0:T(8,128)(2,1)S(1)} %get-tuple-element.118), channel_id=1, source_target_pairs={{0,1},{1,2},{2,3},{3,0},{4,5},{5,6},{6,7},{7,4},{8,9},{9,10},{10,1... | collective-permute-start | bytes 1179656 | tf_op jit(solution)/shard_map/ppermute | solution.py:14
  235.6 23.1 %collective-permute-start.21 = (bf16[192,1024]{1,0:T(8,128)(2,1)S(1)}, bf16[192,1024]{1,0:T(8,128)(2,1)S(1)}, u32[]{:S(2)}, u32[]{:S(2)}) collective-permute-start(bf16[192,1024]{1,0:T(8,128)(2,1)S(1)} %get-tuple-element.120), channel_id=1, source_target_pairs={{0,3},{1,0},{2,1},{3,2},{4,7},{5,4},{6,5},{7,6},{8,11},{9,8},{10,9... | collective-permute-start | bytes 1179656 | tf_op jit(solution)/shard_map/ppermute | solution.py:14
  238.5 27.0 %collective-permute-start.20 = (bf16[192,1024]{1,0:T(8,128)(2,1)S(1)}, bf16[192,1024]{1,0:T(8,128)(2,1)S(1)}, u32[]{:S(2)}, u32[]{:S(2)}) collective-permute-start(bf16[192,1024]{1,0:T(8,128)(2,1)S(1)} %get-tuple-element.122), channel_id=1, source_target_pairs={{0,2},{1,3},{2,0},{3,1},{4,6},{5,7},{6,4},{7,5},{8,10},{9,11},{10,... | collective-permute-start | bytes 1179656 | tf_op jit(solution)/shard_map/ppermute | solution.py:14
  240.0 46.6 %collective-permute-start.38 = (bf16[2,3,64,1152]{3,2,1,0:T(8,128)(2,1)}, bf16[2,3,64,1152]{3,2,1,0:T(8,128)(2,1)}, u32[]{:S(2)}, u32[]{:S(2)}) collective-permute-start(bf16[2,3,64,1152]{3,2,1,0:T(8,128)(2,1)} %pad_maximum_fusion.7), channel_id=1, source_target_pairs={{0,48},{8,56},{16,0},{24,8},{32,16},{40,24},{48,32},{56,40},{64,11... | collective-permute-start | bytes 2654216 | tf_op jit(solution)/shard_map/ppermute | solution.py:22
  242.9 43.8 %collective-permute-start.36 = (bf16[2,3,64,1152]{3,2,1,0:T(8,128)(2,1)}, bf16[2,3,64,1152]{3,2,1,0:T(8,128)(2,1)}, u32[]{:S(2)}, u32[]{:S(2)}) collective-permute-start(bf16[2,3,64,1152]{3,2,1,0:T(8,128)(2,1)} %pad_maximum_fusion.6), channel_id=1, source_target_pairs={{0,16},{8,24},{16,32},{24,40},{32,48},{40,56},{48,0},{56,8},{64,80... | collective-permute-start | bytes 2654216 | tf_op jit(solution)/shard_map/ppermute | solution.py:22
  267.8 12.3 %collective-permute-start.23 = (bf16[192,1024]{1,0:T(8,128)(2,1)S(1)}, bf16[192,1024]{1,0:T(8,128)(2,1)}, u32[]{:S(2)}, u32[]{:S(2)}) collective-permute-start(bf16[192,1024]{1,0:T(8,128)(2,1)S(1)} %get-tuple-element.59), channel_id=1, source_target_pairs={{0,1},{1,2},{2,3},{3,0},{4,5},{5,6},{6,7},{7,4},{8,9},{9,10},{10,1... | collective-permute-start | bytes 1179656 | tf_op jit(solution)/shard_map/ppermute | solution.py:14
  269.7 15.1 %collective-permute-start.24 = (bf16[192,1024]{1,0:T(8,128)(2,1)S(1)}, bf16[192,1024]{1,0:T(8,128)(2,1)}, u32[]{:S(2)}, u32[]{:S(2)}) collective-permute-start(bf16[192,1024]{1,0:T(8,128)(2,1)S(1)} %get-tuple-element.59), channel_id=1, source_target_pairs={{0,3},{1,0},{2,1},{3,2},{4,7},{5,4},{6,5},{7,6},{8,11},{9,8},{10,9... | collective-permute-start | bytes 1179656 | tf_op jit(solution)/shard_map/ppermute | solution.py:14
  271.1 15.5 %collective-permute-start.25 = (bf16[192,1024]{1,0:T(8,128)(2,1)S(1)}, bf16[192,1024]{1,0:T(8,128)(2,1)S(1)}, u32[]{:S(2)}, u32[]{:S(2)}) collective-permute-start(bf16[192,1024]{1,0:T(8,128)(2,1)S(1)} %get-tuple-element.59), channel_id=1, source_target_pairs={{0,2},{1,3},{2,0},{3,1},{4,6},{5,7},{6,4},{7,5},{8,10},{9,11},{10,... | collective-permute-start | bytes 1179656 | tf_op jit(solution)/shard_map/ppermute | solution.py:14
  280.0 14.4 %collective-permute-start.26 = (bf16[528,1024]{1,0:T(8,128)(2,1)S(1)}, bf16[528,1024]{1,0:T(8,128)(2,1)S(1)}, u32[]{:S(2)}, u32[]{:S(2)}) collective-permute-start(bf16[528,1024]{1,0:T(8,128)(2,1)S(1)} %pad_maximum_fusion.5), channel_id=1, source_target_pairs={{0,8},{8,0},{16,24},{24,16},{32,40},{40,32},{48,56},{56,48},{64,72... | collective-permute-start | bytes 3244040 | tf_op jit(solution)/shard_map/ppermute | solution.py:26
  289.3 12.8 %collective-permute-start.39 = (bf16[3,64,1152]{2,1,0:T(8,128)(2,1)S(1)}, bf16[3,64,1152]{2,1,0:T(8,128)(2,1)S(1)}, u32[]{:S(2)}, u32[]{:S(2)}) collective-permute-start(bf16[3,64,1152]{2,1,0:T(8,128)(2,1)S(1)} %dynamic-slice_bitcast_fusion.6), channel_id=1, source_target_pairs={{0,68},{4,64},{8,76},{12,72},{16,84},{20,80},{24,92},{28,88},{32,1... | collective-permute-start | bytes 1327112 | tf_op jit(solution)/shard_map/ppermute | solution.py:34
  295.1 9.2 %collective-permute-start.29 = (bf16[144,1024]{1,0:T(8,128)(2,1)S(1)}, bf16[144,1024]{1,0:T(8,128)(2,1)S(1)}, u32[]{:S(2)}, u32[]{:S(2)}) collective-permute-start(bf16[144,1024]{1,0:T(8,128)(2,1)S(1)} %get-tuple-element.111), channel_id=1, source_target_pairs={{0,48},{8,56},{16,0},{24,8},{32,16},{40,24},{48,32},{56,40},{64,11... | collective-permute-start | bytes 884744 | tf_op jit(solution)/shard_map/ppermute | solution.py:22
  296.6 13.0 %collective-permute-start.28 = (bf16[144,1024]{1,0:T(8,128)(2,1)S(1)}, bf16[144,1024]{1,0:T(8,128)(2,1)S(1)}, u32[]{:S(2)}, u32[]{:S(2)}) collective-permute-start(bf16[144,1024]{1,0:T(8,128)(2,1)S(1)} %get-tuple-element.110), channel_id=1, source_target_pairs={{0,16},{8,24},{16,32},{24,40},{32,48},{40,56},{48,0},{56,8},{64,80... | collective-permute-start | bytes 884744 | tf_op jit(solution)/shard_map/ppermute | solution.py:22
  297.2 12.4 %collective-permute-start.27 = (bf16[144,1024]{1,0:T(8,128)(2,1)S(1)}, bf16[144,1024]{1,0:T(8,128)(2,1)S(1)}, u32[]{:S(2)}, u32[]{:S(2)}) collective-permute-start(bf16[144,1024]{1,0:T(8,128)(2,1)S(1)} %get-tuple-element.109), channel_id=1, source_target_pairs={{0,32},{8,40},{16,48},{24,56},{32,0},{40,8},{48,16},{56,24},{64,96... | collective-permute-start | bytes 884744 | tf_op jit(solution)/shard_map/ppermute | solution.py:22
  302.2 8.9 %collective-permute-start.40 = (bf16[3,64,1152]{2,1,0:T(8,128)(2,1)S(1)}, bf16[3,64,1152]{2,1,0:T(8,128)(2,1)S(1)}, u32[]{:S(2)}, u32[]{:S(2)}) collective-permute-start(bf16[3,64,1152]{2,1,0:T(8,128)(2,1)S(1)} %fusion.40), channel_id=1, source_target_pairs={{0,4},{4,0},{1,5},{5,1},{2,6},{6,2},{3,7},{7,3},{8,12},{12,8},{9,1... | collective-permute-start | bytes 1327112 | tf_op jit(solution)/shard_map/ppermute | solution.py:38
  309.9 6.6 %collective-permute-start.30 = (bf16[80,1024]{1,0:T(8,128)(2,1)S(1)}, bf16[80,1024]{1,0:T(8,128)(2,1)S(1)}, u32[]{:S(2)}, u32[]{:S(2)}) collective-permute-start(bf16[80,1024]{1,0:T(8,128)(2,1)S(1)} %pad_maximum_fusion.16), channel_id=1, source_target_pairs={{0,68},{4,64},{8,76},{12,72},{16,84},{20,80},{24,92},{28,88},{32,1... | collective-permute-start | bytes 491528 | tf_op jit(solution)/shard_map/ppermute | solution.py:34
  316.6 5.4 %collective-permute-start.31 = (bf16[80,1024]{1,0:T(8,128)(2,1)S(1)}, bf16[80,1024]{1,0:T(8,128)(2,1)S(1)}, u32[]{:S(2)}, u32[]{:S(2)}) collective-permute-start(bf16[80,1024]{1,0:T(8,128)(2,1)S(1)} %pad_maximum_fusion.17), channel_id=1, source_target_pairs={{0,4},{4,0},{1,5},{5,1},{2,6},{6,2},{3,7},{7,3},{8,12},{12,8},{9,1... | collective-permute-start | bytes 491528 | tf_op jit(solution)/shard_map/ppermute | solution.py:38
  322.0 5.6 %collective-permute-start.34 = (f32[16,128]{1,0:T(8,128)S(1)}, f32[16,128]{1,0:T(8,128)S(1)}, u32[]{:S(2)}, u32[]{:S(2)}) collective-permute-start(f32[16,128]{1,0:T(8,128)S(1)} %reshape.192), channel_id=1, source_target_pairs={{0,2},{1,3},{2,0},{3,1},{4,6},{5,7},{6,4},{7,5},{8,10},{9,11},{10,... | collective-permute-start | bytes 24584 | tf_op jit(solution)/shard_map/ppermute | solution.py:14
  322.4 5.2 %collective-permute-start.33 = (f32[16,128]{1,0:T(8,128)S(1)}, f32[16,128]{1,0:T(8,128)S(1)}, u32[]{:S(2)}, u32[]{:S(2)}) collective-permute-start(f32[16,128]{1,0:T(8,128)S(1)} %reshape.192), channel_id=1, source_target_pairs={{0,3},{1,0},{2,1},{3,2},{4,7},{5,4},{6,5},{7,6},{8,11},{9,8},{10,9... | collective-permute-start | bytes 24584 | tf_op jit(solution)/shard_map/ppermute | solution.py:14
  325.7 4.9 %collective-permute-start.32 = (f32[16,128]{1,0:T(8,128)S(1)}, f32[16,128]{1,0:T(8,128)S(1)}, u32[]{:S(2)}, u32[]{:S(2)}) collective-permute-start(f32[16,128]{1,0:T(8,128)S(1)} %reshape.192), channel_id=1, source_target_pairs={{0,1},{1,2},{2,3},{3,0},{4,5},{5,6},{6,7},{7,4},{8,9},{9,10},{10,1... | collective-permute-start | bytes 24584 | tf_op jit(solution)/shard_map/ppermute | solution.py:14
  (46 other events, 403.1 us)
Sparse Core Ops, SparseCore 0:
  11.1 72.4 all-gather.1
  184.9 81.0 all-reduce.2
